TPU v7x, 32 devices: a whole 2x2x4 slice. The times are simulated.
32 devices in a mesh: gx: 4 (over z), gy: 4 (over y, x), gz: 2 (over core).
Axes of the slice: x: 2, y: 2, z: 4, core: 2. Of those that a mesh axis runs over, the one named last changes fastest.
Arguments:
- interact: bfloat16 [16, 8192, 512], P(None, ('gx', 'gy', 'gz')), may hold values from -6 to 6
- weight_one: bfloat16 [512, 1024], replicated, may hold values from -0.25 to 0.25
- bias_one: float32 [1024], replicated, may hold values from -3 to 3
- weight_two: bfloat16 [1024, 1024], replicated, may hold values from -0.1875 to 0.1875
- bias_two: float32 [1024], replicated, may hold values from -3 to 3
- weight_three: bfloat16 [1024, 512], replicated, may hold values from -0.1875 to 0.1875
- bias_three: float32 [512], replicated, may hold values from -3 to 3
- weight_four: bfloat16 [512, 256], replicated, may hold values from -0.25 to 0.25
- bias_four: float32 [256], replicated, may hold values from -3 to 3
- weight_out: bfloat16 [256, 1], replicated, may hold values from -1 to 1
- bias_out: float32 [1], replicated, may hold values from -1.5 to 0
- bucket_index: int32 [16, 8192], P(None, ('gx', 'gy', 'gz')), may hold values from 0 to 4095
- labels: int32 [16, 8192], P(None, ('gx', 'gy', 'gz')), may hold values from 0 to 1
Outputs:
- bucket_stats: float32 [16, 4, 4096], P(None, None, 'gx')
- summary: float32 [16, 4], replicated
All inputs are finite; a program needn't handle non-finite values.
Results may differ from a plain program's by a relative error of at most 0.0045.
Values sent between devices are 32-bit elements; how exact they have to be, the bound alone decides.
A program may use at most 128 MiB of HBM per device.

v0:
```python
import jax
import jax.numpy as jnp
from jax import lax
from jax.sharding import PartitionSpec as P

NBUCK = 4096


def layer_relu(inputs, weight, offset):
    return jax.nn.relu(jnp.dot(inputs, weight, preferred_element_type=jnp.float32) + offset).astype(
        jnp.bfloat16
    )


def bucket_reports(totals):
    positives = totals[:, 0]
    negatives = totals[:, 1]
    counts = jnp.maximum(positives + negatives, 1.0)
    return jnp.stack(
        [positives / counts, totals[:, 2] / counts, totals[:, 3] / counts, totals[:, 4] / counts],
        axis=1,
    )


def summarize(numerator, column_sums):
    pair_count = jnp.maximum(column_sums[:, 0] * column_sums[:, 1], 1.0)
    example_count = jnp.maximum(column_sums[:, 0] + column_sums[:, 1], 1.0)
    return jnp.stack(
        [
            numerator / pair_count,
            column_sums[:, 3] / example_count,
            column_sums[:, 2] / jnp.maximum(column_sums[:, 0], 1.0),
            column_sums[:, 4] / example_count,
        ],
        axis=1,
    )


def split_parts(values):
    upper = values.astype(jnp.bfloat16)
    remain = values - upper.astype(jnp.float32)
    middle = remain.astype(jnp.bfloat16)
    lower = (remain - middle.astype(jnp.float32)).astype(jnp.bfloat16)
    return jnp.concatenate([upper, middle, lower], axis=0)


def merge_reports(histograms):
    totals = lax.psum(histograms, ("gx", "gy", "gz"))
    reports = bucket_reports(totals)
    shard_width = totals.shape[2] // lax.axis_size("gx")
    report_block = lax.dynamic_slice_in_dim(
        reports, lax.axis_index("gx") * shard_width, shard_width, 2
    )
    negatives = totals[:, 1]
    below_count = jnp.cumsum(negatives, axis=1) - negatives
    numerator = jnp.sum(totals[:, 0] * (below_count + 0.5 * negatives), axis=1)
    return (report_block, summarize(numerator, jnp.sum(totals, axis=2)))


def on_device(
    interact,
    weight_one,
    bias_one,
    weight_two,
    bias_two,
    weight_three,
    bias_three,
    weight_four,
    bias_four,
    weight_out,
    bias_out,
    bucket_index,
    labels,
):
    intervals, local_rows, features_in = interact.shape
    flat_rows = interact.reshape(intervals * local_rows, features_in)
    hidden = layer_relu(flat_rows, weight_one, bias_one)
    hidden = layer_relu(hidden, weight_two, bias_two)
    hidden = layer_relu(hidden, weight_three, bias_three)
    hidden = layer_relu(hidden, weight_four, bias_four)
    logits = jnp.dot(hidden, weight_out, preferred_element_type=jnp.float32)[:, 0] + bias_out[0]
    logits = logits.reshape(intervals, local_rows)
    observed = labels.astype(jnp.float32)
    predicted = jax.nn.sigmoid(logits)
    losses = jax.nn.softplus(logits) - observed * logits
    squared = (predicted - observed) ** 2
    values = jnp.stack([observed, 1.0 - observed, predicted, losses, squared], axis=1)
    bucket_ids = lax.broadcasted_iota(jnp.int32, (1, NBUCK), 1)

    def histogram_one(inputs):
        row_values, buckets = inputs
        one_hot = (buckets[:, None] == bucket_ids).astype(jnp.bfloat16)
        parts = split_parts(row_values)
        partial_value = jnp.dot(parts, one_hot, preferred_element_type=jnp.float32)
        return jnp.sum(partial_value.reshape(3, row_values.shape[0], NBUCK), axis=0)

    histograms = lax.map(histogram_one, (values, bucket_index))
    bucket_stats, summary = merge_reports(histograms)
    return (bucket_stats, summary)


def solution(mesh):
    in_specs = (
        P(None, ("gx", "gy", "gz"), None),
        P(),
        P(),
        P(),
        P(),
        P(),
        P(),
        P(),
        P(),
        P(),
        P(),
        P(None, ("gx", "gy", "gz")),
        P(None, ("gx", "gy", "gz")),
    )
    out_specs = (P(None, None, "gx"), P())
    return jax.shard_map(
        on_device, mesh=mesh, in_specs=in_specs, out_specs=out_specs, check_vma=False
    )
```

profile of v0, /device:TPU:1, one launch (start us, length us, event | category | flops | bytes accessed | tf_op | source)
XLA Modules:
  0.0 273.3 jit_solution(3193596184140294484)
XLA Ops:
  8.8 18.6 %fusion.11 = f32[4096,1024]{1,0:T(8,128)} fusion(bf16[1024,1024]{1,0:T(8,128)(2,1)S(1)} %copy-done, f32[1024]{0:T(1024)} %param.17, bf16[4096,512]{1,0:T(8,128)(2,1)} %bitcast.66, bf16[512,1024]{1,0:T(8,128)(2,1)} %param.16), kind=kOutput, calls=%fused_computation.17 | convolution fusion | flops 12897484800 | bytes 24121344 | tf_op jit(solution)/shard_map/dot_general | solution.py:10
  27.5 10.5 %fusion.20 = bf16[4096,256]{1,0:T(8,128)(2,1)} fusion(bf16[512,256]{1,0:T(8,128)(2,1)S(1)} %copy-done.5, bf16[1024,512]{1,0:T(8,128)(2,1)S(1)} %copy-done.4, f32[4096,1024]{1,0:T(8,128)} %fusion.11, f32[1024]{0:T(1024)S(1)} %copy-done.6, f32[512]{0:T(512)S(1)} %copy-done.7, f32[256]{0:T(256)S(1)} %copy-done.8), kind=kOutput, calls=%fused_computation.27 | convolution fusion | flops 5390729216 | bytes 20192256 | tf_op jit(solution)/shard_map/dot_general | solution.py:10
  38.0 2.2 fusion.35
  40.6 72.6 %while.11 = (s32[]{:T(128)}, f32[16,5,4096]{2,0,1:T(8,128)}, f32[16,5,256]{2,1,0:T(8,128)S(1)}, s32[16,256]{1,0:T(8,128)}, s32[]{:T(128)}, /*index=5*/f32[]{:T(128)}, s32[]{:T(128)}) while((s32[]{:T(128)}, f32[16,5,4096]{2,0,1:T(8,128)}, f32[16,5,256]{2,1,0:T(8,128)S(1)}, s32[16,256]{1,0:T(8,128)}, s32[]{:T(128)}, ...), condition=%wide.region_2.3_spmd.clone, body=%wide.region_0.2_spmd.clone.sunk | while | flops 32577536 | bytes 1418845 | solution.py:97
  42.3 2.8 %dynamic_update_slice.6 = f32[16,5,4096]{2,0,1:T(8,128)} dynamic-update-slice(f32[16,5,4096]{2,0,1:T(8,128)} %get-tuple-element.107, f32[1,5,4096]{2,0,1:T(1,128)S(1)} %copy.38, s32[]{:T(128)} %get-tuple-element.106, s32[]{:T(128)} %constant.20.clone.1..sunk, s32[]{:T(128)} %constant.20.clone.1..sunk) | dynamic-update-slice | bytes 163844 | tf_op jit(solution)/shard_map/while/body/jit(dynamic_update_index_in_dim)/dynamic_update_slice | solution.py:97
  46.8 2.8 %dynamic_update_slice.6 = f32[16,5,4096]{2,0,1:T(8,128)} dynamic-update-slice(f32[16,5,4096]{2,0,1:T(8,128)} %get-tuple-element.107, f32[1,5,4096]{2,0,1:T(1,128)S(1)} %copy.38, s32[]{:T(128)} %get-tuple-element.106, s32[]{:T(128)} %constant.20.clone.1..sunk, s32[]{:T(128)} %constant.20.clone.1..sunk) | dynamic-update-slice | bytes 163844 | tf_op jit(solution)/shard_map/while/body/jit(dynamic_update_index_in_dim)/dynamic_update_slice | solution.py:97
  51.4 2.8 %dynamic_update_slice.6 = f32[16,5,4096]{2,0,1:T(8,128)} dynamic-update-slice(f32[16,5,4096]{2,0,1:T(8,128)} %get-tuple-element.107, f32[1,5,4096]{2,0,1:T(1,128)S(1)} %copy.38, s32[]{:T(128)} %get-tuple-element.106, s32[]{:T(128)} %constant.20.clone.1..sunk, s32[]{:T(128)} %constant.20.clone.1..sunk) | dynamic-update-slice | bytes 163844 | tf_op jit(solution)/shard_map/while/body/jit(dynamic_update_index_in_dim)/dynamic_update_slice | solution.py:97
  55.9 2.8 %dynamic_update_slice.6 = f32[16,5,4096]{2,0,1:T(8,128)} dynamic-update-slice(f32[16,5,4096]{2,0,1:T(8,128)} %get-tuple-element.107, f32[1,5,4096]{2,0,1:T(1,128)S(1)} %copy.38, s32[]{:T(128)} %get-tuple-element.106, s32[]{:T(128)} %constant.20.clone.1..sunk, s32[]{:T(128)} %constant.20.clone.1..sunk) | dynamic-update-slice | bytes 163844 | tf_op jit(solution)/shard_map/while/body/jit(dynamic_update_index_in_dim)/dynamic_update_slice | solution.py:97
  60.4 2.8 %dynamic_update_slice.6 = f32[16,5,4096]{2,0,1:T(8,128)} dynamic-update-slice(f32[16,5,4096]{2,0,1:T(8,128)} %get-tuple-element.107, f32[1,5,4096]{2,0,1:T(1,128)S(1)} %copy.38, s32[]{:T(128)} %get-tuple-element.106, s32[]{:T(128)} %constant.20.clone.1..sunk, s32[]{:T(128)} %constant.20.clone.1..sunk) | dynamic-update-slice | bytes 163844 | tf_op jit(solution)/shard_map/while/body/jit(dynamic_update_index_in_dim)/dynamic_update_slice | solution.py:97
  65.0 2.8 %dynamic_update_slice.6 = f32[16,5,4096]{2,0,1:T(8,128)} dynamic-update-slice(f32[16,5,4096]{2,0,1:T(8,128)} %get-tuple-element.107, f32[1,5,4096]{2,0,1:T(1,128)S(1)} %copy.38, s32[]{:T(128)} %get-tuple-element.106, s32[]{:T(128)} %constant.20.clone.1..sunk, s32[]{:T(128)} %constant.20.clone.1..sunk) | dynamic-update-slice | bytes 163844 | tf_op jit(solution)/shard_map/while/body/jit(dynamic_update_index_in_dim)/dynamic_update_slice | solution.py:97
  69.5 2.8 %dynamic_update_slice.6 = f32[16,5,4096]{2,0,1:T(8,128)} dynamic-update-slice(f32[16,5,4096]{2,0,1:T(8,128)} %get-tuple-element.107, f32[1,5,4096]{2,0,1:T(1,128)S(1)} %copy.38, s32[]{:T(128)} %get-tuple-element.106, s32[]{:T(128)} %constant.20.clone.1..sunk, s32[]{:T(128)} %constant.20.clone.1..sunk) | dynamic-update-slice | bytes 163844 | tf_op jit(solution)/shard_map/while/body/jit(dynamic_update_index_in_dim)/dynamic_update_slice | solution.py:97
  74.0 2.8 %dynamic_update_slice.6 = f32[16,5,4096]{2,0,1:T(8,128)} dynamic-update-slice(f32[16,5,4096]{2,0,1:T(8,128)} %get-tuple-element.107, f32[1,5,4096]{2,0,1:T(1,128)S(1)} %copy.38, s32[]{:T(128)} %get-tuple-element.106, s32[]{:T(128)} %constant.20.clone.1..sunk, s32[]{:T(128)} %constant.20.clone.1..sunk) | dynamic-update-slice | bytes 163844 | tf_op jit(solution)/shard_map/while/body/jit(dynamic_update_index_in_dim)/dynamic_update_slice | solution.py:97
  78.6 2.8 %dynamic_update_slice.6 = f32[16,5,4096]{2,0,1:T(8,128)} dynamic-update-slice(f32[16,5,4096]{2,0,1:T(8,128)} %get-tuple-element.107, f32[1,5,4096]{2,0,1:T(1,128)S(1)} %copy.38, s32[]{:T(128)} %get-tuple-element.106, s32[]{:T(128)} %constant.20.clone.1..sunk, s32[]{:T(128)} %constant.20.clone.1..sunk) | dynamic-update-slice | bytes 163844 | tf_op jit(solution)/shard_map/while/body/jit(dynamic_update_index_in_dim)/dynamic_update_slice | solution.py:97
  83.1 2.8 %dynamic_update_slice.6 = f32[16,5,4096]{2,0,1:T(8,128)} dynamic-update-slice(f32[16,5,4096]{2,0,1:T(8,128)} %get-tuple-element.107, f32[1,5,4096]{2,0,1:T(1,128)S(1)} %copy.38, s32[]{:T(128)} %get-tuple-element.106, s32[]{:T(128)} %constant.20.clone.1..sunk, s32[]{:T(128)} %constant.20.clone.1..sunk) | dynamic-update-slice | bytes 163844 | tf_op jit(solution)/shard_map/while/body/jit(dynamic_update_index_in_dim)/dynamic_update_slice | solution.py:97
  87.7 2.8 %dynamic_update_slice.6 = f32[16,5,4096]{2,0,1:T(8,128)} dynamic-update-slice(f32[16,5,4096]{2,0,1:T(8,128)} %get-tuple-element.107, f32[1,5,4096]{2,0,1:T(1,128)S(1)} %copy.38, s32[]{:T(128)} %get-tuple-element.106, s32[]{:T(128)} %constant.20.clone.1..sunk, s32[]{:T(128)} %constant.20.clone.1..sunk) | dynamic-update-slice | bytes 163844 | tf_op jit(solution)/shard_map/while/body/jit(dynamic_update_index_in_dim)/dynamic_update_slice | solution.py:97
  92.2 2.8 %dynamic_update_slice.6 = f32[16,5,4096]{2,0,1:T(8,128)} dynamic-update-slice(f32[16,5,4096]{2,0,1:T(8,128)} %get-tuple-element.107, f32[1,5,4096]{2,0,1:T(1,128)S(1)} %copy.38, s32[]{:T(128)} %get-tuple-element.106, s32[]{:T(128)} %constant.20.clone.1..sunk, s32[]{:T(128)} %constant.20.clone.1..sunk) | dynamic-update-slice | bytes 163844 | tf_op jit(solution)/shard_map/while/body/jit(dynamic_update_index_in_dim)/dynamic_update_slice | solution.py:97
  96.7 2.8 %dynamic_update_slice.6 = f32[16,5,4096]{2,0,1:T(8,128)} dynamic-update-slice(f32[16,5,4096]{2,0,1:T(8,128)} %get-tuple-element.107, f32[1,5,4096]{2,0,1:T(1,128)S(1)} %copy.38, s32[]{:T(128)} %get-tuple-element.106, s32[]{:T(128)} %constant.20.clone.1..sunk, s32[]{:T(128)} %constant.20.clone.1..sunk) | dynamic-update-slice | bytes 163844 | tf_op jit(solution)/shard_map/while/body/jit(dynamic_update_index_in_dim)/dynamic_update_slice | solution.py:97
  101.3 2.8 %dynamic_update_slice.6 = f32[16,5,4096]{2,0,1:T(8,128)} dynamic-update-slice(f32[16,5,4096]{2,0,1:T(8,128)} %get-tuple-element.107, f32[1,5,4096]{2,0,1:T(1,128)S(1)} %copy.38, s32[]{:T(128)} %get-tuple-element.106, s32[]{:T(128)} %constant.20.clone.1..sunk, s32[]{:T(128)} %constant.20.clone.1..sunk) | dynamic-update-slice | bytes 163844 | tf_op jit(solution)/shard_map/while/body/jit(dynamic_update_index_in_dim)/dynamic_update_slice | solution.py:97
  105.8 2.8 %dynamic_update_slice.6 = f32[16,5,4096]{2,0,1:T(8,128)} dynamic-update-slice(f32[16,5,4096]{2,0,1:T(8,128)} %get-tuple-element.107, f32[1,5,4096]{2,0,1:T(1,128)S(1)} %copy.38, s32[]{:T(128)} %get-tuple-element.106, s32[]{:T(128)} %constant.20.clone.1..sunk, s32[]{:T(128)} %constant.20.clone.1..sunk) | dynamic-update-slice | bytes 163844 | tf_op jit(solution)/shard_map/while/body/jit(dynamic_update_index_in_dim)/dynamic_update_slice | solution.py:97
  110.3 2.8 %dynamic_update_slice.6 = f32[16,5,4096]{2,0,1:T(8,128)} dynamic-update-slice(f32[16,5,4096]{2,0,1:T(8,128)} %get-tuple-element.107, f32[1,5,4096]{2,0,1:T(1,128)S(1)} %copy.38, s32[]{:T(128)} %get-tuple-element.106, s32[]{:T(128)} %constant.20.clone.1..sunk, s32[]{:T(128)} %constant.20.clone.1..sunk) | dynamic-update-slice | bytes 163844 | tf_op jit(solution)/shard_map/while/body/jit(dynamic_update_index_in_dim)/dynamic_update_slice | solution.py:97
  113.2 132.6 %all-reduce.2.cloned.1.call-done = f32[16,5,4096]{2,0,1:T(8,128)} async-done(((f32[16,5,4096]{2,0,1:T(8,128)}), f32[16,5,4096]{2,0,1:T(8,128)}) %all-reduce.2.cloned.1.call-update) | async-done | bytes 1310736 | tf_op jit(solution)/shard_map/psum | solution.py:48
  245.9 2.0 slice_divide_fusion
  248.7 9.6 %reduce-window.6 = f32[16,32,128]{2,1,0:T(8,128)} reduce-window(f32[16,32,128]{2,1,0:T(8,128)} %bitcast.60, f32[]{:T(128)} %constant.21.clone.1), window={size=1x1x128 pad=0_0x0_0x127_0}, to_apply=%region_4.5 | reduce-window | flops 8323072 | bytes 524292 | tf_op jit(solution)/shard_map/reduce-window
  259.7 1.8 broadcast_add_fusion
  (136 shorter events, 34.9 us)
Async XLA Ops:
  7.2 1.6 copy-start
  7.2 238.7 %all-reduce.2.cloned.1.call-start = ((), (), s32[]{:S(2)}) async-start(), calls=%async_computation | async-start | bytes 2621440 | tf_op jit(solution)/shard_map/psum | solution.py:48
  8.8 18.6 %copy-start.4 = (bf16[1024,512]{1,0:T(8,128)(2,1)S(1)}, bf16[1024,512]{1,0:T(8,128)(2,1)}, u32[]{:S(2)}) copy-start(bf16[1024,512]{1,0:T(8,128)(2,1)} %param.20) | copy-start | bytes 3145732
  8.8 18.6 %copy-start.5 = (bf16[512,256]{1,0:T(8,128)(2,1)S(1)}, bf16[512,256]{1,0:T(8,128)(2,1)}, u32[]{:S(2)}) copy-start(bf16[512,256]{1,0:T(8,128)(2,1)} %param.22) | copy-start | bytes 786436
  8.8 18.6 %copy-start.6 = (f32[1024]{0:T(1024)S(1)}, f32[1024]{0:T(1024)}, u32[]{:S(2)}) copy-start(f32[1024]{0:T(1024)} %param.19) | copy-start | bytes 12292
  8.8 18.6 %copy-start.7 = (f32[512]{0:T(512)S(1)}, f32[512]{0:T(512)}, u32[]{:S(2)}) copy-start(f32[512]{0:T(512)} %param.21) | copy-start | bytes 6148
  8.8 18.6 %copy-start.8 = (f32[256]{0:T(256)S(1)}, f32[256]{0:T(256)}, u32[]{:S(2)}) copy-start(f32[256]{0:T(256)} %param.23) | copy-start | bytes 3076
  27.4 10.6 %copy-start.3 = (bf16[256,1]{0,1:T(2,128)(2,1)S(1)}, bf16[256,1]{0,1:T(2,128)(2,1)}, u32[]{:S(2)}) copy-start(bf16[256,1]{0,1:T(2,128)(2,1)} %param.24) | copy-start | bytes 1540
  27.5 12.8 %copy-start.2 = (s32[16,256]{1,0:T(8,128)S(1)}, s32[16,256]{1,0:T(8,128)}, u32[]{:S(2)}) copy-start(s32[16,256]{1,0:T(8,128)} %param.27) | copy-start | bytes 49156
  245.9 18.6 %copy-start.1 = (f32[16,5,4096]{2,0,1:T(8,128)S(1)}, f32[16,5,4096]{2,0,1:T(8,128)}, u32[]{:S(2)}) copy-start(f32[16,5,4096]{2,0,1:T(8,128)} %all-reduce.2.cloned.1.call-done) | copy-start | bytes 3932164
Sparse Core Ops, SparseCore 0:
  113.3 132.4 all-reduce.1
where the time goes:
time: 277 us; the launch traced here: 273 us
  waiting for transfers between devices  133 us (48%)
  local copies, waits for them, and re-layouts  62.6 us (23%)
  matrix products  44.2 us (16%)
  other arithmetic  18.4 us (7%)
  between operations  15 us (5%)
    psum x1, waiting for transfers between devices, merge_reports(): totals = lax.psum(histograms, ('gx', 'gy', 'gz'))  133 us
    dynamic_update_slice x32, local copies, waits for them, and re-layouts, on_device(): histograms = lax.map(histogram_one, (values, bucket_index))  46.9 us
    dot_general x2, matrix products, layer_relu(): jnp.dot(inputs, weight, preferred_element_type=jnp.float32) + offset  29.1 us
    dot_general x16, matrix products, histogram_one(): partial_value = jnp.dot(parts, one_hot, preferred_element_type=jnp.float32)  12.8 us
    another operation x3, other arithmetic  11.6 us
    dynamic_slice x16, local copies, waits for them, and re-layouts, on_device(): histograms = lax.map(histogram_one, (values, bucket_index))  11.2 us
  transfers between devices with their start and end apart: 1, of which 1 were waited for; matrix products, arithmetic and copies ran while one was open for 0% of the time, Pallas kernels for 0%

commit v1 on v0

v1 whole, which is shorter than its diff:
```python
import functools

import jax
import jax.numpy as jnp
from jax import lax
from jax.experimental import pallas as pl
from jax.experimental.pallas import tpu as pltpu
from jax.sharding import PartitionSpec as P

NBUCK = 4096
LANES = 128
HIGHS = NBUCK // LANES
MESH = pl.DeviceIdType.MESH
AXES = ("gx", "gy", "gz")


def mlp_kernel(
    rows,
    x_ref,
    w1_ref,
    b1_ref,
    w2_ref,
    b2_ref,
    w3_ref,
    b3_ref,
    w4_ref,
    b4_ref,
    wo_ref,
    bo_ref,
    bucket_ref,
    label_ref,
    out_ref,
    h1_ref,
    h2_ref,
    h3_ref,
    h4_ref,
):
    step = pl.program_id(0)

    def layer(src, w_ref, b_ref, dst):
        for col in range(0, w_ref.shape[1], 256):
            cols = slice(col, col + 256)
            acc = jnp.dot(src[...], w_ref[:, cols], preferred_element_type=jnp.float32)
            dst[:, cols] = jnp.maximum(acc + b_ref[:, cols], 0.0).astype(jnp.bfloat16)

    layer(x_ref, w1_ref, b1_ref, h1_ref)
    layer(h1_ref, w2_ref, b2_ref, h2_ref)
    layer(h2_ref, w3_ref, b3_ref, h3_ref)
    layer(h3_ref, w4_ref, b4_ref, h4_ref)
    wide = jnp.broadcast_to(wo_ref[...].astype(jnp.float32), (16, wo_ref.shape[1]))
    logits = lax.dot_general(
        wide.astype(jnp.bfloat16),
        h4_ref[...],
        (((1,), (1,)), ((), ())),
        preferred_element_type=jnp.float32,
    )[0:1] + bo_ref[...]
    per = rows // LANES
    for row in range(x_ref.shape[0] // LANES):
        out_ref[step, 0, row : row + 1, :] = logits[:, row * LANES : (row + 1) * LANES]

    @pl.when(step == 0)
    def _():
        intervals, lines = bucket_ref.shape[0], out_ref.shape[2]
        for i in range(intervals):
            for j in range(per):
                slot, row = divmod(i * per + j, lines)
                cols = slice(j * LANES, (j + 1) * LANES)
                out_ref[slot, 1, row : row + 1, :] = bucket_ref[i : i + 1, cols].astype(
                    jnp.float32
                )
                out_ref[slot, 2, row : row + 1, :] = label_ref[i : i + 1, cols].astype(
                    jnp.float32
                )


def merge_kernel(
    sizes,
    slots,
    packed_ref,
    stats_ref,
    summary_ref,
    got,
    vals,
    hist,
    res,
    send_sem,
    recv_sem,
    res_send_sem,
    res_recv_sem,
):
    nx, ny, nz = sizes
    group = ny * nz
    devices = nx * group
    x, y, z = (lax.axis_index(a) for a in AXES)
    mine = y * nz + z
    me = x * group + mine
    slot = lax.rem(mine, slots)
    copies = mine // slots
    intervals = stats_ref.shape[0]
    held = intervals // slots
    blocks = stats_ref.shape[2]
    rows = packed_ref.shape[2]
    per = rows // held

    def place(d):
        inner = lax.rem(d, group)
        return (d // group, inner // nz, lax.rem(inner, nz))

    barrier = pltpu.get_barrier_semaphore()

    @pl.loop(1, devices)
    def _(k):
        d = lax.rem(me + k, devices)
        pl.semaphore_signal(barrier, inc=1, device_id=place(d), device_id_type=MESH)

    pl.semaphore_wait(barrier, devices - 1)

    @pl.loop(1, devices)
    def _(k):
        d = lax.rem(me + k, devices)
        pltpu.make_async_remote_copy(
            src_ref=packed_ref.at[lax.rem(lax.rem(d, group), slots)],
            dst_ref=got.at[me],
            send_sem=send_sem,
            recv_sem=recv_sem,
            device_id=place(d),
            device_id_type=MESH,
        ).start()

    pltpu.make_async_copy(packed_ref.at[slot], got.at[me], recv_sem).start()
    pltpu.make_async_copy(got, got, recv_sem).wait()

    logit = got[:, 0]
    label = got[:, 2]
    small = jnp.exp(-jnp.abs(logit))
    predicted = jnp.where(logit >= 0.0, 1.0, small) / (1.0 + small)
    losses = jnp.maximum(logit, 0.0) + jnp.log1p(small) - label * logit
    squared = (predicted - label) ** 2
    vals[:, 0] = predicted
    vals[:, 1] = losses
    vals[:, 2] = squared

    width = per * LANES
    low_ids = lax.broadcasted_iota(jnp.int32, (LANES, width), 0)
    high_ids = lax.broadcasted_iota(jnp.int32, (HIGHS, width), 0)
    block_ids = lax.broadcasted_iota(jnp.int32, (blocks, width), 0) + x * blocks
    tall = 2 * HIGHS + 6 * blocks

    def add(n, totals):
        out = []
        for i in range(held):
            def line(ref, k):
                return jnp.concatenate(
                    [ref[n, k, i * per + j : i * per + j + 1, :] for j in range(per)], axis=1
                )

            bucket = line(got, 1).astype(jnp.int32)
            observed = line(got, 2)
            low = bucket & (LANES - 1)
            high = lax.shift_right_logical(bucket, LANES.bit_length() - 1)
            one_hot = jnp.where(low_ids == low, 1.0, 0.0).astype(jnp.bfloat16)
            at_high = high_ids == high
            at_block = block_ids == high
            parts = [
                jnp.where(at_high, observed, 0.0),
                jnp.where(at_high, 1.0 - observed, 0.0),
            ]
            lower = []
            for k in range(3):
                value = line(vals, k)
                upper = value.astype(jnp.bfloat16).astype(jnp.float32)
                parts.append(jnp.where(at_block, upper, 0.0))
                lower.append(jnp.where(at_block, value - upper, 0.0))
            left = jnp.concatenate(parts + lower, axis=0).astype(jnp.bfloat16)
            out.append(
                totals[i]
                + lax.dot_general(
                    left, one_hot, (((1,), (1,)), ((), ())), preferred_element_type=jnp.float32
                )
            )
        return tuple(out)

    zero = jnp.zeros((tall, LANES), jnp.float32)
    totals = lax.fori_loop(0, devices, add, (zero,) * held)

    before = lax.broadcasted_iota(jnp.int32, (LANES, LANES), 0)
    after = lax.broadcasted_iota(jnp.int32, (LANES, LANES), 1)
    lane_before = jnp.where(before < after, 1.0, 0.0)
    row_before = jnp.where(
        lax.broadcasted_iota(jnp.int32, (HIGHS, HIGHS), 0)
        > lax.broadcasted_iota(jnp.int32, (HIGHS, HIGHS), 1),
        1.0,
        0.0,
    )
    lane_ids = lax.broadcasted_iota(jnp.int32, (8, LANES), 1)
    exact = functools.partial(
        jnp.dot, preferred_element_type=jnp.float32, precision=lax.Precision.HIGHEST
    )

    def whole_sum(a):
        return jnp.sum(jnp.sum(a, axis=0, keepdims=True), axis=1, keepdims=True)

    for i in range(held):
        total = totals[i]
        hist[...] = total[: 2 * HIGHS]
        own = pl.ds(pl.multiple_of(x * blocks, blocks), blocks)
        own_neg = pl.ds(pl.multiple_of(HIGHS + x * blocks, blocks), blocks)
        positives, negatives = hist[own, :], hist[own_neg, :]
        count = jnp.maximum(positives + negatives, 1.0)
        at = slot * held + i
        res[at, 0:blocks, :] = positives / count
        for k in range(3):
            first = 2 * HIGHS + k * blocks
            second = first + 3 * blocks
            value = total[first : first + blocks] + total[second : second + blocks]
            res[at, (k + 1) * blocks : (k + 2) * blocks, :] = value / count
        pos, neg = total[:HIGHS], total[HIGHS : 2 * HIGHS]
        rows_below = jnp.sum(exact(row_before, neg), axis=1, keepdims=True)
        below = exact(neg, lane_before) + rows_below
        numerator = whole_sum(pos * (below + 0.5 * neg))
        p_sum, n_sum = whole_sum(pos), whole_sum(neg)
        sums = []
        for k in range(3):
            part = jnp.sum(vals[:, k, i * per : (i + 1) * per, :], axis=0)
            sums.append(whole_sum(part))
        examples = jnp.maximum(p_sum + n_sum, 1.0)
        line = jnp.where(lane_ids == 0, numerator / jnp.maximum(p_sum * n_sum, 1.0), 0.0)
        line = jnp.where(lane_ids == 1, sums[1] / examples, line)
        line = jnp.where(lane_ids == 2, sums[0] / jnp.maximum(p_sum, 1.0), line)
        line = jnp.where(lane_ids == 3, sums[2] / examples, line)
        res[at, 4 * blocks : 4 * blocks + 8, :] = line

    here = pl.ds(slot * held, held)

    @pl.loop(1, slots)
    def _(k):
        d = x * group + copies * slots + lax.rem(slot + k, slots)
        pltpu.make_async_remote_copy(
            src_ref=res.at[here],
            dst_ref=res.at[here],
            send_sem=res_send_sem,
            recv_sem=res_recv_sem,
            device_id=place(d),
            device_id_type=MESH,
        ).start()

    others = res.at[pl.ds(0, intervals - held)]
    if slots > 1:
        pltpu.make_async_copy(others, others, res_recv_sem).wait()
    for k in range(4):
        stats_ref[:, k] = res[:, k * blocks : (k + 1) * blocks, :]
    summary_ref[...] = res[:, 4 * blocks : 4 * blocks + 8, :]
    if slots > 1:
        pltpu.make_async_copy(others, others, res_send_sem).wait()
    if devices > 1:
        sent = got.at[pl.ds(0, devices - 1)]
        pltpu.make_async_copy(sent, sent, send_sem).wait()


def on_device(
    sizes,
    interact,
    weight_one,
    bias_one,
    weight_two,
    bias_two,
    weight_three,
    bias_three,
    weight_four,
    bias_four,
    weight_out,
    bias_out,
    bucket_index,
    labels,
):
    intervals, rows, features = interact.shape
    nx, ny, nz = sizes
    devices = nx * ny * nz
    slots = min(ny * nz, intervals)
    held = intervals // slots
    tile = held * rows
    lines = tile // LANES
    blocks = HIGHS // nx
    flat = interact.reshape(intervals * rows, features)
    wide = [w.shape[1] for w in (weight_one, weight_two, weight_three, weight_four)]

    def whole(a):
        return pl.BlockSpec(a.shape, lambda s: (0,) * a.ndim)

    operands = [
        weight_one,
        bias_one.reshape(1, -1),
        weight_two,
        bias_two.reshape(1, -1),
        weight_three,
        bias_three.reshape(1, -1),
        weight_four,
        bias_four.reshape(1, -1),
        weight_out.reshape(1, -1),
        bias_out.reshape(1, 1),
        bucket_index,
        labels,
    ]
    packed = pl.pallas_call(
        functools.partial(mlp_kernel, rows),
        grid=(slots,),
        in_specs=[pl.BlockSpec((tile, features), lambda s: (s, 0))]
        + [whole(a) for a in operands],
        out_specs=pl.BlockSpec((slots, 3, lines, LANES), lambda s: (0, 0, 0, 0)),
        out_shape=jax.ShapeDtypeStruct((slots, 3, lines, LANES), jnp.float32),
        scratch_shapes=[pltpu.VMEM((tile, w), jnp.bfloat16) for w in wide],
        compiler_params=pltpu.CompilerParams(vmem_limit_bytes=40 * 2**20),
        name="top_mlp",
    )(flat, *operands)

    vmem = pl.BlockSpec(memory_space=pltpu.VMEM)
    stats, summary = pl.pallas_call(
        functools.partial(merge_kernel, sizes, slots),
        in_specs=[vmem],
        out_specs=[vmem, vmem],
        out_shape=[
            jax.ShapeDtypeStruct((intervals, 4, blocks, LANES), jnp.float32),
            jax.ShapeDtypeStruct((intervals, 8, LANES), jnp.float32),
        ],
        scratch_shapes=[
            pltpu.VMEM((devices, 3, lines, LANES), jnp.float32),
            pltpu.VMEM((devices, 3, lines, LANES), jnp.float32),
            pltpu.VMEM((2 * HIGHS, LANES), jnp.float32),
            pltpu.VMEM((intervals, 4 * blocks + 8, LANES), jnp.float32),
            pltpu.SemaphoreType.DMA,
            pltpu.SemaphoreType.DMA,
            pltpu.SemaphoreType.DMA,
            pltpu.SemaphoreType.DMA,
        ],
        compiler_params=pltpu.CompilerParams(
            collective_id=0, has_side_effects=True, vmem_limit_bytes=24 * 2**20
        ),
        name="merge_buckets",
    )(packed)
    return stats.reshape(intervals, 4, blocks * LANES), summary[:, 0, :4]


def solution(mesh):
    sizes = tuple(mesh.shape[a] for a in AXES)
    in_specs = (
        (P(None, AXES, None),) + (P(),) * 10 + (P(None, AXES), P(None, AXES))
    )
    out_specs = (P(None, None, "gx"), P())
    return jax.shard_map(
        functools.partial(on_device, sizes),
        mesh=mesh,
        in_specs=in_specs,
        out_specs=out_specs,
        check_vma=False,
    )
```

time: 277 us -> 61 us (0.22); the launches traced: 273 us -> 60.5 us
  waiting for transfers between devices: 133 us -> 0 us
  local copies, waits for them, and re-layouts: 62.6 us -> 13.5 us
  Pallas kernels: 0 us -> 45.7 us
  matrix products: 44.2 us -> 0 us
  other arithmetic: 18.4 us -> 0 us
  between operations: 15 us -> 1.31 us
    psum x1 -> x0, waiting for transfers between devices: 133 us -> none  [merge_reports(): totals = lax.psum(histograms, ('gx', 'gy', 'gz'))]
    dynamic_update_slice x32 -> x0, local copies, waits for them, and re-layouts: 46.9 us -> none  [on_device(): histograms = lax.map(histogram_one, (values, bucket_index))]
    pallas_call x0 -> x2, Pallas kernels: none -> 45.7 us  [the longest x1 24 us: on_device(): pl.pallas_call(functools.partial(merge_kernel, sizes, slots), in_specs=[v...]
    dot_general x19 -> x0, matrix products: 44.2 us -> none  [the longest x2 29.1 us: layer_relu(): jnp.dot(inputs, weight, preferred_element_type=jnp.float32) + offset]
    another operation x6 -> x0, other arithmetic: 13 us -> none
    dynamic_slice x16 -> x0, local copies, waits for them, and re-layouts: 11.2 us -> none  [on_device(): histograms = lax.map(histogram_one, (values, bucket_index))]
    unnamed x20 -> x24, local copies, waits for them, and re-layouts: 2.43 us -> 12 us
    div x4 -> x0, other arithmetic: 3.34 us -> none  [the longest x1 2.05 us: bucket_reports(): totals[:, 4] / counts]
  transfers between devices with their start and end apart: 1 -> 0, of which waited for: 1 -> 0; matrix products, arithmetic and copies ran while one was open for 0% -> 0% of each run, Pallas kernels for 0% -> 0%
where the time goes in v1:
time: 61 us; the launch traced here: 60.5 us
  Pallas kernels  45.7 us (75%)
  local copies, waits for them, and re-layouts  13.5 us (22%)
  between operations  1.31 us (2%)
    pallas_call x1, Pallas kernels, on_device(): pl.pallas_call(functools.partial(merge_kernel, sizes, slots), in_specs=[v...  24 us
    pallas_call x1, Pallas kernels, on_device(): pl.pallas_call(functools.partial(mlp_kernel, rows), grid=(slots,), in_spe...  21.7 us
    unnamed x24, local copies, waits for them, and re-layouts  12 us

profile of v1, /device:TPU:1, one launch (start us, length us, event | category | flops | bytes accessed | tf_op | source)
XLA Modules:
  0.0 60.5 jit_solution(4788006877622314844)
XLA Ops:
  1.3 0.0 copy-start
  1.3 2.2 %copy-done = bf16[16,256,512]{2,1,0:T(8,128)(2,1)S(1)} copy-done((bf16[16,256,512]{2,1,0:T(8,128)(2,1)S(1)}, bf16[16,256,512]{2,1,0:T(8,128)(2,1)}, u32[]{:S(2)}) %copy-start) | copy-done | bytes 4194328
  3.5 0.0 copy-start.1
  3.5 1.6 %copy-done.1 = bf16[1024,1024]{1,0:T(8,128)(2,1)S(1)} copy-done((bf16[1024,1024]{1,0:T(8,128)(2,1)S(1)}, bf16[1024,1024]{1,0:T(8,128)(2,1)}, u32[]{:S(2)}) %copy-start.1) | copy-done | bytes 2097176
  5.1 0.0 copy-start.2
  5.1 1.2 %copy-done.2 = bf16[512,1024]{1,0:T(8,128)(2,1)S(1)} copy-done((bf16[512,1024]{1,0:T(8,128)(2,1)S(1)}, bf16[512,1024]{1,0:T(8,128)(2,1)}, u32[]{:S(2)}) %copy-start.2) | copy-done | bytes 1048600
  6.3 0.0 copy-start.3
  6.3 1.2 %copy-done.3 = bf16[1024,512]{1,0:T(8,128)(2,1)S(1)} copy-done((bf16[1024,512]{1,0:T(8,128)(2,1)S(1)}, bf16[1024,512]{1,0:T(8,128)(2,1)}, u32[]{:S(2)}) %copy-start.3) | copy-done | bytes 1048600
  7.5 0.0 copy-start.4
  7.5 0.9 %copy-done.4 = bf16[512,256]{1,0:T(8,128)(2,1)S(1)} copy-done((bf16[512,256]{1,0:T(8,128)(2,1)S(1)}, bf16[512,256]{1,0:T(8,128)(2,1)}, u32[]{:S(2)}) %copy-start.4) | copy-done | bytes 262168
  8.5 0.0 copy-start.5
  8.5 0.7 %copy-done.5 = s32[16,256]{1,0:T(8,128)S(1)} copy-done((s32[16,256]{1,0:T(8,128)S(1)}, s32[16,256]{1,0:T(8,128)}, u32[]{:S(2)}) %copy-start.5) | copy-done | bytes 16408
  9.2 0.0 copy-start.6
  9.2 0.7 %copy-done.6 = s32[16,256]{1,0:T(8,128)S(1)} copy-done((s32[16,256]{1,0:T(8,128)S(1)}, s32[16,256]{1,0:T(8,128)}, u32[]{:S(2)}) %copy-start.6) | copy-done | bytes 16408
  9.9 0.0 copy-start.7
  9.9 0.7 %copy-done.7 = f32[1024]{0:T(1024)S(1)} copy-done((f32[1024]{0:T(1024)S(1)}, f32[1024]{0:T(1024)}, u32[]{:S(2)}) %copy-start.7) | copy-done | bytes 4120
  10.6 0.7 %copy-done.8 = f32[1024]{0:T(1024)S(1)} copy-done((f32[1024]{0:T(1024)S(1)}, f32[1024]{0:T(1024)}, u32[]{:S(2)}) %copy-start.8) | copy-done | bytes 4120
  11.3 0.7 %copy-done.9 = f32[512]{0:T(512)S(1)} copy-done((f32[512]{0:T(512)S(1)}, f32[512]{0:T(512)}, u32[]{:S(2)}) %copy-start.9) | copy-done | bytes 2072
  12.0 0.7 %copy-done.10 = f32[256]{0:T(256)S(1)} copy-done((f32[256]{0:T(256)S(1)}, f32[256]{0:T(256)}, u32[]{:S(2)}) %copy-start.10) | copy-done | bytes 1048
  12.6 0.7 %copy-done.11 = bf16[256,1]{0,1:T(2,128)(2,1)S(1)} copy-done((bf16[256,1]{0,1:T(2,128)(2,1)S(1)}, bf16[256,1]{0,1:T(2,128)(2,1)}, u32[]{:S(2)}) %copy-start.11) | copy-done | bytes 536
  13.3 21.7 %top_mlp.1.packed_ref = f32[8,3,4,128]{3,2,1,0:T(4,128)S(1)} custom-call(bf16[4096,512]{1,0:T(8,128)(2,1)S(1)} %bitcast.11, bf16[512,1024]{1,0:T(8,128)(2,1)S(1)} %copy-done.2, f32[1,1024]{1,0:T(1,128)S(1)} %bitcast.12, bf16[1024,1024]{1,0:T(8,128)(2,1)S(1)} %copy-done.1, f32[1,1024]{1,0:T(1,128)S(1)} %bitcast.13, bf16[1024,512]{1,0:T(8,128)(2,1)S(1)} %copy-done.3, ...), custom_call_target="tpu_custom_call" | custom-call | tf_op jit(solution)/shard_map/top_mlp/pallas_call | solution.py:304
  35.0 24.0 %merge_buckets.1 = (f32[16,4,8,128]{3,2,1,0:T(8,128)S(1)}, f32[16,8,128]{2,1,0:T(8,128)S(1)}) custom-call(f32[8,3,4,128]{3,2,1,0:T(4,128)S(1)} %top_mlp.1.packed_ref), custom_call_target="tpu_custom_call" | custom-call | tf_op jit(solution)/shard_map/merge_buckets/pallas_call | solution.py:317
  59.1 0.8 %reshape.35 = f32[16,4,1024]{2,1,0:T(4,128)} reshape(f32[16,4,8,128]{3,2,1,0:T(8,128)S(1)} %get-tuple-element.4) | data formatting | bytes 524288 | tf_op jit(solution)/shard_map/reshape | solution.py:340
  59.9 0.7 %copy.15 = f32[16,1,4]{0,2,1:T(4,128)} copy(f32[16,1,4]{2,1,0:T(1,128)S(1)} %slice.3) | data formatting | bytes 512 | tf_op jit(solution)/shard_map/slice | solution.py:340
  (5 shorter events, 0.0 us)
Async XLA Ops:
  1.3 2.2 %copy-start = (bf16[16,256,512]{2,1,0:T(8,128)(2,1)S(1)}, bf16[16,256,512]{2,1,0:T(8,128)(2,1)}, u32[]{:S(2)}) copy-start(bf16[16,256,512]{2,1,0:T(8,128)(2,1)} %param.13) | copy-start | bytes 12582916
  3.5 1.6 %copy-start.1 = (bf16[1024,1024]{1,0:T(8,128)(2,1)S(1)}, bf16[1024,1024]{1,0:T(8,128)(2,1)}, u32[]{:S(2)}) copy-start(bf16[1024,1024]{1,0:T(8,128)(2,1)} %w2_ref.1) | copy-start | bytes 6291460
  5.1 1.2 %copy-start.2 = (bf16[512,1024]{1,0:T(8,128)(2,1)S(1)}, bf16[512,1024]{1,0:T(8,128)(2,1)}, u32[]{:S(2)}) copy-start(bf16[512,1024]{1,0:T(8,128)(2,1)} %w1_ref.1) | copy-start | bytes 3145732
  6.3 1.2 %copy-start.3 = (bf16[1024,512]{1,0:T(8,128)(2,1)S(1)}, bf16[1024,512]{1,0:T(8,128)(2,1)}, u32[]{:S(2)}) copy-start(bf16[1024,512]{1,0:T(8,128)(2,1)} %w3_ref.1) | copy-start | bytes 3145732
  7.5 0.9 %copy-start.4 = (bf16[512,256]{1,0:T(8,128)(2,1)S(1)}, bf16[512,256]{1,0:T(8,128)(2,1)}, u32[]{:S(2)}) copy-start(bf16[512,256]{1,0:T(8,128)(2,1)} %w4_ref.1) | copy-start | bytes 786436
  8.5 0.7 %copy-start.5 = (s32[16,256]{1,0:T(8,128)S(1)}, s32[16,256]{1,0:T(8,128)}, u32[]{:S(2)}) copy-start(s32[16,256]{1,0:T(8,128)} %bucket_ref.1) | copy-start | bytes 49156
  9.2 0.7 %copy-start.6 = (s32[16,256]{1,0:T(8,128)S(1)}, s32[16,256]{1,0:T(8,128)}, u32[]{:S(2)}) copy-start(s32[16,256]{1,0:T(8,128)} %label_ref.1) | copy-start | bytes 49156
  9.9 0.7 %copy-start.7 = (f32[1024]{0:T(1024)S(1)}, f32[1024]{0:T(1024)}, u32[]{:S(2)}) copy-start(f32[1024]{0:T(1024)} %param.15) | copy-start | bytes 12292
  10.6 0.7 %copy-start.8 = (f32[1024]{0:T(1024)S(1)}, f32[1024]{0:T(1024)}, u32[]{:S(2)}) copy-start(f32[1024]{0:T(1024)} %param.17) | copy-start | bytes 12292
  11.3 0.7 %copy-start.9 = (f32[512]{0:T(512)S(1)}, f32[512]{0:T(512)}, u32[]{:S(2)}) copy-start(f32[512]{0:T(512)} %param.19) | copy-start | bytes 6148
  12.0 0.7 %copy-start.10 = (f32[256]{0:T(256)S(1)}, f32[256]{0:T(256)}, u32[]{:S(2)}) copy-start(f32[256]{0:T(256)} %param.21) | copy-start | bytes 3076
  12.6 0.7 %copy-start.11 = (bf16[256,1]{0,1:T(2,128)(2,1)S(1)}, bf16[256,1]{0,1:T(2,128)(2,1)}, u32[]{:S(2)}) copy-start(bf16[256,1]{0,1:T(2,128)(2,1)} %param.22) | copy-start | bytes 1540

commit v2 on v1

v2 whole, which is shorter than its diff:
```python
import functools

import jax
import jax.numpy as jnp
from jax import lax
from jax.experimental import pallas as pl
from jax.experimental.pallas import tpu as pltpu
from jax.sharding import PartitionSpec as P

NBUCK = 4096
LANES = 128
PAIR = 2
HIGHS = NBUCK // LANES
MESH = pl.DeviceIdType.MESH
AXES = ("gx", "gy", "gz")


def exact_digits(a, bound):
    digits, scale = [], 1.0
    while True:
        if bound <= 256:
            return digits + [(a, scale)]
        upper = jnp.floor(a * (1.0 / 256.0))
        digits.append((a - 256.0 * upper, scale))
        a, bound, scale = upper, bound // 256, scale * 256.0


def report_kernel(
    sizes,
    slots,
    x_hbm,
    w1_hbm,
    b1_hbm,
    w2_hbm,
    b2_hbm,
    w3_hbm,
    b3_hbm,
    w4_hbm,
    b4_hbm,
    wo_hbm,
    bo_ref,
    bucket_hbm,
    label_hbm,
    stats_ref,
    summary_ref,
    x_ref,
    w1_ref,
    b1_ref,
    w2_ref,
    b2_ref,
    w3_ref,
    b3_ref,
    w4_ref,
    b4_ref,
    wo_ref,
    bucket_ref,
    label_ref,
    hidden_one,
    hidden_two,
    hidden_three,
    hidden_four,
    packed,
    got,
    vals,
    hist,
    res,
    x_sem,
    w_sem,
    send_sem,
    recv_sem,
    res_send_sem,
    res_recv_sem,
):
    nx, ny, nz = sizes
    group = ny * nz
    devices = nx * group
    x, y, z = (lax.axis_index(a) for a in AXES)
    mine = y * nz + z
    me = x * group + mine
    slot = lax.rem(mine, slots)
    own_copy = mine // slots
    copies = group // slots
    intervals = stats_ref.shape[0]
    held = intervals // slots
    blocks = stats_ref.shape[2]
    tile = x_ref.shape[1]
    lines = tile // LANES
    per = lines // held

    def place(d):
        inner = lax.rem(d, group)
        return (d // group, inner // nz, lax.rem(inner, nz))

    def turn(i):
        return lax.rem(slot + 1 + i, slots)

    loads = {}
    pairs = (
        ("w1", w1_hbm, w1_ref),
        ("b1", b1_hbm, b1_ref),
        ("w2", w2_hbm, w2_ref),
        ("b2", b2_hbm, b2_ref),
        ("w3", w3_hbm, w3_ref),
        ("b3", b3_hbm, b3_ref),
        ("w4", w4_hbm, w4_ref),
        ("b4", b4_hbm, b4_ref),
        ("wo", wo_hbm, wo_ref),
        ("bucket", bucket_hbm, bucket_ref),
        ("label", label_hbm, label_ref),
    )

    def x_load(i):
        at = turn(i)
        return pltpu.make_async_copy(x_hbm.at[at], x_ref.at[at], x_sem.at[i])

    x_load(0).start()
    for k, (key, src, dst) in enumerate(pairs):
        loads[key] = pltpu.make_async_copy(src, dst, w_sem.at[k])
        loads[key].start()
        if key == "b1":
            for i in range(1, PAIR if slots % PAIR == 0 else 1):
                x_load(i).start()
    for i in range(PAIR if slots % PAIR == 0 else 1, slots):
        x_load(i).start()

    barrier = pltpu.get_barrier_semaphore()

    @pl.loop(1, devices)
    def _(k):
        d = lax.rem(me + k, devices)
        pl.semaphore_signal(barrier, inc=1, device_id=place(d), device_id_type=MESH)

    def layer(src, w_ref, b_ref, dst):
        for col in range(0, w_ref.shape[1], 256):
            cols = slice(col, col + 256)
            acc = jnp.dot(src[...], w_ref[:, cols], preferred_element_type=jnp.float32)
            dst[:, cols] = jnp.maximum(acc + b_ref[:, cols], 0.0).astype(jnp.bfloat16)

    def scores(order, first):
        def need(*keys):
            if first:
                for key in keys:
                    loads[key].wait()

        where = [turn(i) for i in order]
        for i in order:
            x_load(i).wait()
        need("w1", "b1")
        for p, c in enumerate(where):
            layer(x_ref.at[c], w1_ref, b1_ref, hidden_one.at[p])
        need("w2", "b2")
        for p, c in enumerate(where):
            layer(hidden_one.at[p], w2_ref, b2_ref, hidden_two.at[p])
        need("w3", "b3")
        for p, c in enumerate(where):
            layer(hidden_two.at[p], w3_ref, b3_ref, hidden_three.at[p])
        need("w4", "b4")
        for p, c in enumerate(where):
            layer(hidden_three.at[p], w4_ref, b4_ref, hidden_four.at[p])
        need("wo")
        wide = jnp.broadcast_to(wo_ref[...].astype(jnp.float32), (16, wo_ref.shape[1]))
        for p, c in enumerate(where):
            logits = lax.dot_general(
                wide.astype(jnp.bfloat16),
                hidden_four[p],
                (((1,), (1,)), ((), ())),
                preferred_element_type=jnp.float32,
            )[0:1] + bo_ref[0]
            for row in range(lines):
                packed[c, 0, row : row + 1, :] = logits[:, row * LANES : (row + 1) * LANES]

    def send(c):
        here = x * copies + own_copy
        for k in range(nx * copies):
            rep = lax.rem(here + k, nx * copies)
            inner = lax.rem(rep, copies) * slots + c
            remote = pltpu.make_async_remote_copy(
                src_ref=packed.at[c],
                dst_ref=got.at[me],
                send_sem=send_sem,
                recv_sem=recv_sem,
                device_id=(rep // copies, inner // nz, lax.rem(inner, nz)),
                device_id_type=MESH,
            )
            if k == 0:
                pl.when(c != slot)(remote.start)
            else:
                remote.start()

    pair = PAIR if slots % PAIR == 0 else 1
    scores(range(pair), True)

    loads["bucket"].wait()
    loads["label"].wait()
    for i in range(intervals):
        for j in range(per):
            c, row = divmod(i * per + j, lines)
            cols = slice(j * LANES, (j + 1) * LANES)
            packed[c, 1, row : row + 1, :] = bucket_ref[i : i + 1, cols].astype(jnp.float32)
            packed[c, 2, row : row + 1, :] = label_ref[i : i + 1, cols].astype(jnp.float32)

    pl.semaphore_wait(barrier, devices - 1)
    for i in range(pair):
        send(turn(i))

    @pl.loop(1, slots // pair)
    def _(step):
        order = [step * pair + p for p in range(pair)]
        scores(order, False)
        for i in order:
            send(turn(i))

    pltpu.make_async_copy(packed.at[slot], got.at[me], recv_sem).start()
    pltpu.make_async_copy(got, got, recv_sem).wait()

    logit = got[:, 0]
    label = got[:, 2]
    small = jnp.exp(-jnp.abs(logit))
    predicted = jnp.where(logit >= 0.0, 1.0, small) / (1.0 + small)
    losses = jnp.maximum(logit, 0.0) + jnp.log1p(small) - label * logit
    squared = (predicted - label) ** 2
    vals[:, 0] = predicted
    vals[:, 1] = losses
    vals[:, 2] = squared

    batch = next(b for b in (8, 4, 2, 1) if devices % b == 0)
    width = batch * per * LANES
    low_ids = lax.broadcasted_iota(jnp.int32, (LANES, width), 0)
    high_ids = lax.broadcasted_iota(jnp.int32, (HIGHS, width), 0)
    block_ids = lax.broadcasted_iota(jnp.int32, (blocks, width), 0) + x * blocks
    tall = 2 * HIGHS + 6 * blocks

    def add(step, totals):
        out = []
        for i in range(held):

            def line(ref, k):
                return jnp.concatenate(
                    [
                        ref[step * batch + n, k, row : row + 1, :]
                        for n in range(batch)
                        for row in range(i * per, (i + 1) * per)
                    ],
                    axis=1,
                )

            bucket = line(got, 1).astype(jnp.int32)
            observed = line(got, 2)
            low = bucket & (LANES - 1)
            high = lax.shift_right_logical(bucket, LANES.bit_length() - 1)
            one_hot = jnp.where(low_ids == low, 1.0, 0.0).astype(jnp.bfloat16)
            at_high = high_ids == high
            at_block = block_ids == high
            parts = [
                jnp.where(at_high, observed, 0.0),
                jnp.where(at_high, 1.0 - observed, 0.0),
            ]
            lower = []
            for k in range(3):
                value = line(vals, k)
                upper = value.astype(jnp.bfloat16).astype(jnp.float32)
                parts.append(jnp.where(at_block, upper, 0.0))
                lower.append(jnp.where(at_block, value - upper, 0.0))
            left = jnp.concatenate(parts + lower, axis=0).astype(jnp.bfloat16)
            out.append(
                totals[i]
                + lax.dot_general(
                    left, one_hot, (((1,), (1,)), ((), ())), preferred_element_type=jnp.float32
                )
            )
        return tuple(out)

    zero = jnp.zeros((tall, LANES), jnp.float32)
    totals = lax.fori_loop(0, devices // batch, add, (zero,) * held)

    def below_than(size, lower_first):
        a = lax.broadcasted_iota(jnp.int32, (size, size), 0)
        b = lax.broadcasted_iota(jnp.int32, (size, size), 1)
        return jnp.where(a < b if lower_first else b < a, 1.0, 0.0).astype(jnp.bfloat16)

    lane_before = below_than(LANES, True)
    row_before = below_than(HIGHS, False)
    lane_ids = lax.broadcasted_iota(jnp.int32, (8, LANES), 1)
    bound = devices * per * LANES

    for i in range(held):
        total = totals[i]
        at = slot * held + i
        hist[...] = total[: 2 * HIGHS]
        own = pl.ds(pl.multiple_of(x * blocks, blocks), blocks)
        own_neg = pl.ds(pl.multiple_of(HIGHS + x * blocks, blocks), blocks)
        positives, negatives = hist[own, :], hist[own_neg, :]
        count = jnp.maximum(positives + negatives, 1.0)
        res[at, 0:blocks, :] = positives / count
        for k in range(3):
            first = 2 * HIGHS + k * blocks
            second = first + 3 * blocks
            value = total[first : first + blocks] + total[second : second + blocks]
            res[at, (k + 1) * blocks : (k + 2) * blocks, :] = value / count
        pos, neg = total[:HIGHS], total[HIGHS : 2 * HIGHS]
        lane_below = jnp.zeros((HIGHS, LANES), jnp.float32)
        rows_below = jnp.zeros((HIGHS, LANES), jnp.float32)
        for digit, scale in exact_digits(neg, bound):
            digit = digit.astype(jnp.bfloat16)
            lane_below += scale * jnp.dot(
                digit, lane_before, preferred_element_type=jnp.float32
            )
            rows_below += scale * jnp.dot(
                row_before, digit, preferred_element_type=jnp.float32
            )
        below = lane_below + jnp.sum(rows_below, axis=1, keepdims=True)
        sums = [pos * (below + 0.5 * neg), pos, neg]
        sums = [jnp.sum(a, axis=0, keepdims=True) for a in sums]
        for k in range(3):
            part = jnp.sum(vals[:, k, i * per : (i + 1) * per, :], axis=0)
            sums.append(jnp.sum(part, axis=0, keepdims=True))
        sums += [jnp.zeros((1, LANES), jnp.float32)] * 2
        sums = jnp.sum(jnp.concatenate(sums, axis=0), axis=1, keepdims=True)
        numerator, p_sum, n_sum, s_p, s_loss, s_sq = (sums[k : k + 1] for k in range(6))
        examples = jnp.maximum(p_sum + n_sum, 1.0)
        line = jnp.where(lane_ids == 0, numerator / jnp.maximum(p_sum * n_sum, 1.0), 0.0)
        line = jnp.where(lane_ids == 1, s_loss / examples, line)
        line = jnp.where(lane_ids == 2, s_p / jnp.maximum(p_sum, 1.0), line)
        line = jnp.where(lane_ids == 3, s_sq / examples, line)
        res[at, 4 * blocks : 4 * blocks + 8, :] = line

    here = pl.ds(slot * held, held)

    @pl.loop(1, slots)
    def _(k):
        d = x * group + own_copy * slots + lax.rem(slot + k, slots)
        pltpu.make_async_remote_copy(
            src_ref=res.at[here],
            dst_ref=res.at[here],
            send_sem=res_send_sem,
            recv_sem=res_recv_sem,
            device_id=place(d),
            device_id_type=MESH,
        ).start()

    others = res.at[pl.ds(0, intervals - held)]
    if slots > 1:
        pltpu.make_async_copy(others, others, res_recv_sem).wait()
    for k in range(4):
        stats_ref[:, k] = res[:, k * blocks : (k + 1) * blocks, :]
    summary_ref[...] = res[:, 4 * blocks : 4 * blocks + 8, :]
    if slots > 1:
        pltpu.make_async_copy(others, others, res_send_sem).wait()
    if devices > 1:
        sent = got.at[pl.ds(0, devices - 1)]
        pltpu.make_async_copy(sent, sent, send_sem).wait()


def on_device(sizes, *args):
    (
        interact,
        weight_one,
        bias_one,
        weight_two,
        bias_two,
        weight_three,
        bias_three,
        weight_four,
        bias_four,
        weight_out,
        bias_out,
        bucket_index,
        labels,
    ) = args
    intervals, rows, features = interact.shape
    nx, ny, nz = sizes
    devices = nx * ny * nz
    slots = min(ny * nz, intervals)
    pair = PAIR if slots % PAIR == 0 else 1
    held = intervals // slots
    tile = held * rows
    lines = tile // LANES
    blocks = HIGHS // nx
    weights = (weight_one, weight_two, weight_three, weight_four)
    operands = [
        interact.reshape(slots, tile, features),
        weight_one,
        bias_one.reshape(1, -1),
        weight_two,
        bias_two.reshape(1, -1),
        weight_three,
        bias_three.reshape(1, -1),
        weight_four,
        bias_four.reshape(1, -1),
        weight_out.reshape(1, -1),
        bias_out,
        bucket_index,
        labels,
    ]
    vmem = pl.BlockSpec(memory_space=pltpu.VMEM)
    in_specs = [pl.BlockSpec(memory_space=pltpu.HBM)] * len(operands)
    in_specs[10] = pl.BlockSpec(memory_space=pltpu.SMEM)
    stats, summary = pl.pallas_call(
        functools.partial(report_kernel, sizes, slots),
        in_specs=in_specs,
        out_specs=[vmem, vmem],
        out_shape=[
            jax.ShapeDtypeStruct((intervals, 4, blocks, LANES), jnp.float32),
            jax.ShapeDtypeStruct((intervals, 8, LANES), jnp.float32),
        ],
        scratch_shapes=[pltpu.VMEM(a.shape, a.dtype) for k, a in enumerate(operands) if k != 10]
        + [pltpu.VMEM((pair, tile, w.shape[1]), jnp.bfloat16) for w in weights]
        + [
            pltpu.VMEM((slots, 3, lines, LANES), jnp.float32),
            pltpu.VMEM((devices, 3, lines, LANES), jnp.float32),
            pltpu.VMEM((devices, 3, lines, LANES), jnp.float32),
            pltpu.VMEM((2 * HIGHS, LANES), jnp.float32),
            pltpu.VMEM((intervals, 4 * blocks + 8, LANES), jnp.float32),
            pltpu.SemaphoreType.DMA((slots,)),
            pltpu.SemaphoreType.DMA((11,)),
            pltpu.SemaphoreType.DMA,
            pltpu.SemaphoreType.DMA,
            pltpu.SemaphoreType.DMA,
            pltpu.SemaphoreType.DMA,
        ],
        compiler_params=pltpu.CompilerParams(
            collective_id=0, has_side_effects=True, vmem_limit_bytes=56 * 2**20
        ),
        name="report",
    )(*operands)
    return stats.reshape(intervals, 4, blocks * LANES), summary[:, 0, :4]


def solution(mesh):
    sizes = tuple(mesh.shape[a] for a in AXES)
    in_specs = (
        (P(None, AXES, None),) + (P(),) * 10 + (P(None, AXES), P(None, AXES))
    )
    out_specs = (P(None, None, "gx"), P())
    return jax.shard_map(
        functools.partial(on_device, sizes),
        mesh=mesh,
        in_specs=in_specs,
        out_specs=out_specs,
        check_vma=False,
    )
```

time: 61 us -> 44 us (0.72)
  local copies, waits for them, and re-layouts: 13.5 us -> 3.24 us
  Pallas kernels: 45.7 us -> 39.3 us
    unnamed x24 -> x0, local copies, waits for them, and re-layouts: 12 us -> none
    pallas_call x2 -> x1, Pallas kernels: 45.7 us -> 39.3 us  [on_device(): pl.pallas_call(functools.partial(report_kernel, sizes, slots), in_specs=i...]
    reshape x1, local copies, waits for them, and re-layouts: 0.79 us -> 1.74 us  [on_device(): return (stats.reshape(intervals, 4, blocks * LANES), summary[:, 0, :4])]
    slice x2, local copies, waits for them, and re-layouts: 0.66 us -> 1.5 us  [on_device(): return (stats.reshape(intervals, 4, blocks * LANES), summary[:, 0, :4])]
where the time goes in v2:
time: 44 us; the launch traced here: 43.8 us
  Pallas kernels  39.3 us (89%)
  local copies, waits for them, and re-layouts  3.24 us (7%)
  between operations  1.29 us (3%)
    pallas_call x1, Pallas kernels, on_device(): pl.pallas_call(functools.partial(report_kernel, sizes, slots), in_specs=i...  39.3 us
    reshape x1, local copies, waits for them, and re-layouts, on_device(): return (stats.reshape(intervals, 4, blocks * LANES), summary[:, 0, :4])  1.74 us
    slice x2, local copies, waits for them, and re-layouts, on_device(): return (stats.reshape(intervals, 4, blocks * LANES), summary[:, 0, :4])  1.5 us

profile of v2, /device:TPU:1, one launch (start us, length us, event | category | flops | bytes accessed | tf_op | source)
XLA Modules:
  0.0 43.8 jit_solution(13142100648525685486)
XLA Ops:
  1.3 39.3 %report.1 = (f32[16,4,8,128]{3,2,1,0:T(8,128)}, f32[16,8,128]{2,1,0:T(8,128)}) custom-call(bf16[8,512,512]{2,1,0:T(8,128)(2,1)} %bitcast.9, bf16[512,1024]{1,0:T(8,128)(2,1)} %w1_hbm.1, f32[1,1024]{1,0:T(1,128)} %bitcast.10, bf16[1024,1024]{1,0:T(8,128)(2,1)} %w2_hbm.1, f32[1,1024]{1,0:T(1,128)} %bitcast.11, bf16[1024,512]{1,0:T(8,128)(2,1)} %w3_hbm.1, ...), custom_call_target="tpu_custom_call" | custom-call | tf_op jit(solution)/shard_map/report/pallas_call | solution.py:398
  40.6 1.7 %reshape.31 = f32[16,4,1024]{2,1,0:T(4,128)} reshape(f32[16,4,8,128]{3,2,1,0:T(8,128)} %get-tuple-element.4) | data formatting | bytes 524288 | tf_op jit(solution)/shard_map/reshape | solution.py:426
  42.3 0.8 %slice.3 = f32[16,1,4]{2,1,0:T(1,128)S(1)} slice(f32[16,8,128]{2,1,0:T(8,128)} %get-tuple-element.5), slice={[0:16], [0:1], [0:4]} | slice | bytes 512 | tf_op jit(solution)/shard_map/slice | solution.py:426
  43.1 0.7 %copy.15 = f32[16,1,4]{0,2,1:T(4,128)} copy(f32[16,1,4]{2,1,0:T(1,128)S(1)} %slice.3) | data formatting | bytes 512 | tf_op jit(solution)/shard_map/slice | solution.py:426

commit v3 on v2

--- a/solution.py
+++ b/solution.py
@@ -62,7 +62,7 @@
     packed,
     got,
     vals,
-    hist,
+    totals,
     res,
     x_sem,
     w_sem,
@@ -70,6 +70,7 @@
     recv_sem,
     res_send_sem,
     res_recv_sem,
+    out_sem,
 ):
     nx, ny, nz = sizes
     group = ny * nz
@@ -82,10 +83,14 @@
     copies = group // slots
     intervals = stats_ref.shape[0]
     held = intervals // slots
-    blocks = stats_ref.shape[2]
+    span = stats_ref.shape[2]
+    blocks = span // LANES
     tile = x_ref.shape[1]
     lines = tile // LANES
     per = lines // held
+    reps = nx * copies
+    here = x * copies + own_copy
+    pair = PAIR if slots % PAIR == 0 else 1
 
     def place(d):
         inner = lax.rem(d, group)
@@ -136,7 +141,7 @@
             acc = jnp.dot(src[...], w_ref[:, cols], preferred_element_type=jnp.float32)
             dst[:, cols] = jnp.maximum(acc + b_ref[:, cols], 0.0).astype(jnp.bfloat16)
 
-    def scores(order, first):
+    def scores(order, first, beside=()):
         def need(*keys):
             if first:
                 for key in keys:
@@ -150,7 +155,13 @@
             layer(x_ref.at[c], w1_ref, b1_ref, hidden_one.at[p])
         need("w2", "b2")
         for p, c in enumerate(where):
+            if p == len(where) - 1:
+                for i in beside:
+                    arrived(i)
             layer(hidden_one.at[p], w2_ref, b2_ref, hidden_two.at[p])
+            if p == len(where) - 1:
+                for i in beside:
+                    add(i)
         need("w3", "b3")
         for p, c in enumerate(where):
             layer(hidden_two.at[p], w3_ref, b3_ref, hidden_three.at[p])
@@ -169,16 +180,16 @@
             for row in range(lines):
                 packed[c, 0, row : row + 1, :] = logits[:, row * LANES : (row + 1) * LANES]
 
-    def send(c):
-        here = x * copies + own_copy
-        for k in range(nx * copies):
-            rep = lax.rem(here + k, nx * copies)
+    def send(i):
+        c = turn(i)
+        for k in range(reps):
+            rep = lax.rem(here + k, reps)
             inner = lax.rem(rep, copies) * slots + c
             remote = pltpu.make_async_remote_copy(
                 src_ref=packed.at[c],
-                dst_ref=got.at[me],
-                send_sem=send_sem,
-                recv_sem=recv_sem,
+                dst_ref=got.at[i, here],
+                send_sem=send_sem.at[i],
+                recv_sem=recv_sem.at[i],
                 device_id=(rep // copies, inner // nz, lax.rem(inner, nz)),
                 device_id_type=MESH,
             )
@@ -187,59 +198,30 @@
             else:
                 remote.start()
 
-    pair = PAIR if slots % PAIR == 0 else 1
-    scores(range(pair), True)
-
-    loads["bucket"].wait()
-    loads["label"].wait()
-    for i in range(intervals):
-        for j in range(per):
-            c, row = divmod(i * per + j, lines)
-            cols = slice(j * LANES, (j + 1) * LANES)
-            packed[c, 1, row : row + 1, :] = bucket_ref[i : i + 1, cols].astype(jnp.float32)
-            packed[c, 2, row : row + 1, :] = label_ref[i : i + 1, cols].astype(jnp.float32)
-
-    pl.semaphore_wait(barrier, devices - 1)
-    for i in range(pair):
-        send(turn(i))
-
-    @pl.loop(1, slots // pair)
-    def _(step):
-        order = [step * pair + p for p in range(pair)]
-        scores(order, False)
-        for i in order:
-            send(turn(i))
-
-    pltpu.make_async_copy(packed.at[slot], got.at[me], recv_sem).start()
-    pltpu.make_async_copy(got, got, recv_sem).wait()
-
-    logit = got[:, 0]
-    label = got[:, 2]
-    small = jnp.exp(-jnp.abs(logit))
-    predicted = jnp.where(logit >= 0.0, 1.0, small) / (1.0 + small)
-    losses = jnp.maximum(logit, 0.0) + jnp.log1p(small) - label * logit
-    squared = (predicted - label) ** 2
-    vals[:, 0] = predicted
-    vals[:, 1] = losses
-    vals[:, 2] = squared
-
-    batch = next(b for b in (8, 4, 2, 1) if devices % b == 0)
-    width = batch * per * LANES
+    def arrived(i):
+        pltpu.make_async_copy(got.at[i], got.at[i], recv_sem.at[i]).wait()
+
+    width = reps * per * LANES
     low_ids = lax.broadcasted_iota(jnp.int32, (LANES, width), 0)
     high_ids = lax.broadcasted_iota(jnp.int32, (HIGHS, width), 0)
     block_ids = lax.broadcasted_iota(jnp.int32, (blocks, width), 0) + x * blocks
-    tall = 2 * HIGHS + 6 * blocks
-
-    def add(step, totals):
-        out = []
-        for i in range(held):
+
+    def add(i):
+        logit = got[i, :, 0]
+        label = got[i, :, 2]
+        small = jnp.exp(-jnp.abs(logit))
+        predicted = jnp.where(logit >= 0.0, 1.0, small) / (1.0 + small)
+        vals[i, :, 0] = predicted
+        vals[i, :, 1] = jnp.maximum(logit, 0.0) + jnp.log1p(small) - label * logit
+        vals[i, :, 2] = (predicted - label) ** 2
+        for e in range(held):
 
             def line(ref, k):
                 return jnp.concatenate(
                     [
-                        ref[step * batch + n, k, row : row + 1, :]
-                        for n in range(batch)
-                        for row in range(i * per, (i + 1) * per)
+                        ref[i, n, k, row : row + 1, :]
+                        for n in range(reps)
+                        for row in range(e * per, (e + 1) * per)
                     ],
                     axis=1,
                 )
@@ -262,16 +244,38 @@
                 parts.append(jnp.where(at_block, upper, 0.0))
                 lower.append(jnp.where(at_block, value - upper, 0.0))
             left = jnp.concatenate(parts + lower, axis=0).astype(jnp.bfloat16)
-            out.append(
-                totals[i]
-                + lax.dot_general(
-                    left, one_hot, (((1,), (1,)), ((), ())), preferred_element_type=jnp.float32
-                )
+            totals[e] += lax.dot_general(
+                left, one_hot, (((1,), (1,)), ((), ())), preferred_element_type=jnp.float32
             )
-        return tuple(out)
-
-    zero = jnp.zeros((tall, LANES), jnp.float32)
-    totals = lax.fori_loop(0, devices // batch, add, (zero,) * held)
+
+    totals[...] = jnp.zeros_like(totals)
+    scores(range(pair), True)
+
+    loads["bucket"].wait()
+    loads["label"].wait()
+    for i in range(intervals):
+        for j in range(per):
+            c, row = divmod(i * per + j, lines)
+            cols = slice(j * LANES, (j + 1) * LANES)
+            packed[c, 1, row : row + 1, :] = bucket_ref[i : i + 1, cols].astype(jnp.float32)
+            packed[c, 2, row : row + 1, :] = label_ref[i : i + 1, cols].astype(jnp.float32)
+
+    pl.semaphore_wait(barrier, devices - 1)
+    for i in range(pair):
+        send(i)
+
+    @pl.loop(1, slots // pair)
+    def _(step):
+        order = [step * pair + p for p in range(pair)]
+        scores(order, False, [i - pair for i in order])
+        for i in order:
+            send(i)
+
+    last = slots - 1
+    pltpu.make_async_copy(packed.at[slot], got.at[last, here], recv_sem.at[last]).start()
+    for i in range(slots - pair, slots):
+        arrived(i)
+        add(i)
 
     def below_than(size, lower_first):
         a = lax.broadcasted_iota(jnp.int32, (size, size), 0)
@@ -283,20 +287,36 @@
     lane_ids = lax.broadcasted_iota(jnp.int32, (8, LANES), 1)
     bound = devices * per * LANES
 
+    def share(at):
+        @pl.loop(1, slots)
+        def _(k):
+            d = x * group + own_copy * slots + lax.rem(slot + k, slots)
+            pltpu.make_async_remote_copy(
+                src_ref=res.at[at],
+                dst_ref=res.at[at],
+                send_sem=res_send_sem,
+                recv_sem=res_recv_sem,
+                device_id=place(d),
+                device_id_type=MESH,
+            ).start()
+
     for i in range(held):
         total = totals[i]
         at = slot * held + i
-        hist[...] = total[: 2 * HIGHS]
         own = pl.ds(pl.multiple_of(x * blocks, blocks), blocks)
         own_neg = pl.ds(pl.multiple_of(HIGHS + x * blocks, blocks), blocks)
-        positives, negatives = hist[own, :], hist[own_neg, :]
+        positives, negatives = totals[i, own, :], totals[i, own_neg, :]
         count = jnp.maximum(positives + negatives, 1.0)
-        res[at, 0:blocks, :] = positives / count
+        report = [positives / count]
         for k in range(3):
             first = 2 * HIGHS + k * blocks
             second = first + 3 * blocks
             value = total[first : first + blocks] + total[second : second + blocks]
-            res[at, (k + 1) * blocks : (k + 2) * blocks, :] = value / count
+            report.append(value / count)
+        for k in range(4):
+            res[at, k : k + 1, 0:span] = jnp.concatenate(
+                [report[k][h : h + 1] for h in range(blocks)], axis=1
+            )
         pos, neg = total[:HIGHS], total[HIGHS : 2 * HIGHS]
         lane_below = jnp.zeros((HIGHS, LANES), jnp.float32)
         rows_below = jnp.zeros((HIGHS, LANES), jnp.float32)
@@ -312,7 +332,7 @@
         sums = [pos * (below + 0.5 * neg), pos, neg]
         sums = [jnp.sum(a, axis=0, keepdims=True) for a in sums]
         for k in range(3):
-            part = jnp.sum(vals[:, k, i * per : (i + 1) * per, :], axis=0)
+            part = jnp.sum(vals[:, :, k, i * per : (i + 1) * per, :], axis=(0, 1))
             sums.append(jnp.sum(part, axis=0, keepdims=True))
         sums += [jnp.zeros((1, LANES), jnp.float32)] * 2
         sums = jnp.sum(jnp.concatenate(sums, axis=0), axis=1, keepdims=True)
@@ -322,33 +342,23 @@
         line = jnp.where(lane_ids == 1, s_loss / examples, line)
         line = jnp.where(lane_ids == 2, s_p / jnp.maximum(p_sum, 1.0), line)
         line = jnp.where(lane_ids == 3, s_sq / examples, line)
-        res[at, 4 * blocks : 4 * blocks + 8, :] = line
-
-    here = pl.ds(slot * held, held)
-
-    @pl.loop(1, slots)
-    def _(k):
-        d = x * group + own_copy * slots + lax.rem(slot + k, slots)
-        pltpu.make_async_remote_copy(
-            src_ref=res.at[here],
-            dst_ref=res.at[here],
-            send_sem=res_send_sem,
-            recv_sem=res_recv_sem,
-            device_id=place(d),
-            device_id_type=MESH,
-        ).start()
+        res[at, :, span:] = line[0:4]
+        share(at)
 
     others = res.at[pl.ds(0, intervals - held)]
     if slots > 1:
         pltpu.make_async_copy(others, others, res_recv_sem).wait()
-    for k in range(4):
-        stats_ref[:, k] = res[:, k * blocks : (k + 1) * blocks, :]
-    summary_ref[...] = res[:, 4 * blocks : 4 * blocks + 8, :]
+    reports = pltpu.make_async_copy(res.at[:, :, pl.ds(0, span)], stats_ref, out_sem)
+    reports.start()
+    summary_ref[...] = res[:, 0:1, span:]
+    reports.wait()
     if slots > 1:
         pltpu.make_async_copy(others, others, res_send_sem).wait()
-    if devices > 1:
-        sent = got.at[pl.ds(0, devices - 1)]
-        pltpu.make_async_copy(sent, sent, send_sem).wait()
+    for i in range(slots):
+        count = reps - 1 if i == last else reps
+        if count:
+            sent = got.at[i, pl.ds(0, count)]
+            pltpu.make_async_copy(sent, sent, send_sem.at[i]).wait()
 
 
 def on_device(sizes, *args):
@@ -376,6 +386,7 @@
     tile = held * rows
     lines = tile // LANES
     blocks = HIGHS // nx
+    reps = devices // slots
     weights = (weight_one, weight_two, weight_three, weight_four)
     operands = [
         interact.reshape(slots, tile, features),
@@ -398,32 +409,33 @@
     stats, summary = pl.pallas_call(
         functools.partial(report_kernel, sizes, slots),
         in_specs=in_specs,
-        out_specs=[vmem, vmem],
+        out_specs=[pl.BlockSpec(memory_space=pltpu.HBM), vmem],
         out_shape=[
-            jax.ShapeDtypeStruct((intervals, 4, blocks, LANES), jnp.float32),
-            jax.ShapeDtypeStruct((intervals, 8, LANES), jnp.float32),
+            jax.ShapeDtypeStruct((intervals, 4, blocks * LANES), jnp.float32),
+            jax.ShapeDtypeStruct((intervals, 1, LANES), jnp.float32),
         ],
         scratch_shapes=[pltpu.VMEM(a.shape, a.dtype) for k, a in enumerate(operands) if k != 10]
         + [pltpu.VMEM((pair, tile, w.shape[1]), jnp.bfloat16) for w in weights]
         + [
             pltpu.VMEM((slots, 3, lines, LANES), jnp.float32),
-            pltpu.VMEM((devices, 3, lines, LANES), jnp.float32),
-            pltpu.VMEM((devices, 3, lines, LANES), jnp.float32),
-            pltpu.VMEM((2 * HIGHS, LANES), jnp.float32),
-            pltpu.VMEM((intervals, 4 * blocks + 8, LANES), jnp.float32),
+            pltpu.VMEM((slots, reps, 3, lines, LANES), jnp.float32),
+            pltpu.VMEM((slots, reps, 3, lines, LANES), jnp.float32),
+            pltpu.VMEM((held, 2 * HIGHS + 6 * blocks, LANES), jnp.float32),
+            pltpu.VMEM((intervals, 4, (blocks + 1) * LANES), jnp.float32),
             pltpu.SemaphoreType.DMA((slots,)),
             pltpu.SemaphoreType.DMA((11,)),
-            pltpu.SemaphoreType.DMA,
+            pltpu.SemaphoreType.DMA((slots,)),
+            pltpu.SemaphoreType.DMA((slots,)),
             pltpu.SemaphoreType.DMA,
             pltpu.SemaphoreType.DMA,
             pltpu.SemaphoreType.DMA,
         ],
         compiler_params=pltpu.CompilerParams(
-            collective_id=0, has_side_effects=True, vmem_limit_bytes=56 * 2**20
+            collective_id=0, has_side_effects=True, vmem_limit_bytes=60 * 2**20
         ),
         name="report",
     )(*operands)
-    return stats.reshape(intervals, 4, blocks * LANES), summary[:, 0, :4]
+    return stats, summary[:, 0, :4]
 
 
 def solution(mesh):

time: 44 us -> 49.6 us (1.13)
  Pallas kernels: 39.3 us -> 44.8 us
    pallas_call x1, Pallas kernels: 39.3 us -> 44.8 us  [on_device(): pl.pallas_call(functools.partial(report_kernel, sizes, slots), in_specs=i...]
    reshape x1 -> x0, local copies, waits for them, and re-layouts: 1.74 us -> none  [on_device(): return (stats.reshape(intervals, 4, blocks * LANES), summary[:, 0, :4])]
    unnamed x0 -> x1, local copies, waits for them, and re-layouts: none -> 1.67 us
    slice x2 -> x1, local copies, waits for them, and re-layouts: 1.5 us -> 1.35 us  [on_device(): return (stats, summary[:, 0, :4])]
where the time goes in v3:
time: 49.6 us; the launch traced here: 49.1 us
  Pallas kernels  44.8 us (90%)
  local copies, waits for them, and re-layouts  3.02 us (6%)
  between operations  1.29 us (3%)
    pallas_call x1, Pallas kernels, on_device(): pl.pallas_call(functools.partial(report_kernel, sizes, slots), in_specs=i...  44.8 us
    unnamed x1, local copies, waits for them, and re-layouts  1.67 us
    slice x1, local copies, waits for them, and re-layouts, on_device(): return (stats, summary[:, 0, :4])  1.35 us

profile of v3, /device:TPU:1, one launch (start us, length us, event | category | flops | bytes accessed | tf_op | source)
XLA Modules:
  0.0 49.1 jit_solution(15580826181216556058)
XLA Ops:
  1.3 44.8 %report.1 = (f32[16,4,1024]{2,1,0:T(4,128)}, f32[16,1,128]{2,1,0:T(1,128)}) custom-call(bf16[8,512,512]{2,1,0:T(8,128)(2,1)} %bitcast.8, bf16[512,1024]{1,0:T(8,128)(2,1)} %w1_hbm.1, f32[1,1024]{1,0:T(1,128)} %bitcast.10, bf16[1024,1024]{1,0:T(8,128)(2,1)} %w2_hbm.1, f32[1,1024]{1,0:T(1,128)} %bitcast.11, bf16[1024,512]{1,0:T(8,128)(2,1)} %w3_hbm.1, ...), custom_call_target="tpu_custom_call" | custom-call | tf_op jit(solution)/shard_map/report/pallas_call | solution.py:409
  46.1 1.3 %copy.15 = f32[16,1,4]{0,2,1:T(4,128)} copy(f32[16,1,4]{2,1,0:T(1,128)} %bitcast.9) | data formatting | bytes 512 | tf_op jit(solution)/shard_map/slice | solution.py:438
  47.4 1.7 %copy.18 = f32[16,4,1024]{2,1,0:T(4,128)} copy(f32[16,4,1024]{2,1,0:T(4,128)} %get-tuple-element.8) | data formatting | bytes 524288

commit v4 on v3

--- a/solution.py
+++ b/solution.py
@@ -141,7 +141,7 @@
             acc = jnp.dot(src[...], w_ref[:, cols], preferred_element_type=jnp.float32)
             dst[:, cols] = jnp.maximum(acc + b_ref[:, cols], 0.0).astype(jnp.bfloat16)
 
-    def scores(order, first, beside=()):
+    def scores(order, first):
         def need(*keys):
             if first:
                 for key in keys:
@@ -155,13 +155,7 @@
             layer(x_ref.at[c], w1_ref, b1_ref, hidden_one.at[p])
         need("w2", "b2")
         for p, c in enumerate(where):
-            if p == len(where) - 1:
-                for i in beside:
-                    arrived(i)
             layer(hidden_one.at[p], w2_ref, b2_ref, hidden_two.at[p])
-            if p == len(where) - 1:
-                for i in beside:
-                    add(i)
         need("w3", "b3")
         for p, c in enumerate(where):
             layer(hidden_two.at[p], w3_ref, b3_ref, hidden_three.at[p])
@@ -201,36 +195,50 @@
     def arrived(i):
         pltpu.make_async_copy(got.at[i], got.at[i], recv_sem.at[i]).wait()
 
-    width = reps * per * LANES
-    low_ids = lax.broadcasted_iota(jnp.int32, (LANES, width), 0)
+    turns = next(b for b in (max(8 // reps, 1), 1) if slots % b == 0)
+    sources = [(t, n) for t in range(turns) for n in range(reps)]
+    width = len(sources) * per * LANES
+    low_ids = lax.broadcasted_iota(jnp.int32, (LANES, LANES), 1)
     high_ids = lax.broadcasted_iota(jnp.int32, (HIGHS, width), 0)
     block_ids = lax.broadcasted_iota(jnp.int32, (blocks, width), 0) + x * blocks
 
-    def add(i):
-        logit = got[i, :, 0]
-        label = got[i, :, 2]
+    def measure_all():
+        logit = got[:, :, 0]
+        label = got[:, :, 2]
         small = jnp.exp(-jnp.abs(logit))
         predicted = jnp.where(logit >= 0.0, 1.0, small) / (1.0 + small)
-        vals[i, :, 0] = predicted
-        vals[i, :, 1] = jnp.maximum(logit, 0.0) + jnp.log1p(small) - label * logit
-        vals[i, :, 2] = (predicted - label) ** 2
+        vals[:, :, 0] = predicted
+        vals[:, :, 1] = jnp.maximum(logit, 0.0) + jnp.log1p(small) - label * logit
+        vals[:, :, 2] = (predicted - label) ** 2
+
+    def add(step, carry):
+        first = step * turns
+        ids = jnp.concatenate([got[first + t, n, 1] for t, n in sources], axis=0)
+        down = jnp.transpose(ids).astype(jnp.int32) & (LANES - 1)
+        out = []
         for e in range(held):
 
             def line(ref, k):
                 return jnp.concatenate(
                     [
-                        ref[i, n, k, row : row + 1, :]
-                        for n in range(reps)
+                        ref[first + t, n, k, row : row + 1, :]
+                        for t, n in sources
                         for row in range(e * per, (e + 1) * per)
                     ],
                     axis=1,
                 )
 
+            columns = [
+                q * lines + row
+                for q in range(len(sources))
+                for row in range(e * per, (e + 1) * per)
+            ]
+            one_hot = jnp.concatenate(
+                [jnp.where(low_ids == down[:, c : c + 1], 1.0, 0.0) for c in columns], axis=0
+            ).astype(jnp.bfloat16)
             bucket = line(got, 1).astype(jnp.int32)
             observed = line(got, 2)
-            low = bucket & (LANES - 1)
             high = lax.shift_right_logical(bucket, LANES.bit_length() - 1)
-            one_hot = jnp.where(low_ids == low, 1.0, 0.0).astype(jnp.bfloat16)
             at_high = high_ids == high
             at_block = block_ids == high
             parts = [
@@ -244,11 +252,11 @@
                 parts.append(jnp.where(at_block, upper, 0.0))
                 lower.append(jnp.where(at_block, value - upper, 0.0))
             left = jnp.concatenate(parts + lower, axis=0).astype(jnp.bfloat16)
-            totals[e] += lax.dot_general(
-                left, one_hot, (((1,), (1,)), ((), ())), preferred_element_type=jnp.float32
+            out.append(
+                carry[e] + jnp.dot(left, one_hot, preferred_element_type=jnp.float32)
             )
-
-    totals[...] = jnp.zeros_like(totals)
+        return tuple(out)
+
     scores(range(pair), True)
 
     loads["bucket"].wait()
@@ -267,15 +275,19 @@
     @pl.loop(1, slots // pair)
     def _(step):
         order = [step * pair + p for p in range(pair)]
-        scores(order, False, [i - pair for i in order])
+        scores(order, False)
         for i in order:
             send(i)
 
     last = slots - 1
     pltpu.make_async_copy(packed.at[slot], got.at[last, here], recv_sem.at[last]).start()
-    for i in range(slots - pair, slots):
+    for i in range(slots):
         arrived(i)
-        add(i)
+    measure_all()
+    zero = jnp.zeros(totals.shape[1:], jnp.float32)
+    sums = lax.fori_loop(0, slots // turns, add, (zero,) * held)
+    for e in range(held):
+        totals[e] = sums[e]
 
     def below_than(size, lower_first):
         a = lax.broadcasted_iota(jnp.int32, (size, size), 0)
@@ -350,7 +362,19 @@
         pltpu.make_async_copy(others, others, res_recv_sem).wait()
     reports = pltpu.make_async_copy(res.at[:, :, pl.ds(0, span)], stats_ref, out_sem)
     reports.start()
-    summary_ref[...] = res[:, 0:1, span:]
+    pick = jnp.where(
+        lax.broadcasted_iota(jnp.int32, (8, LANES), 0)
+        == lax.broadcasted_iota(jnp.int32, (8, LANES), 1),
+        1.0,
+        0.0,
+    )
+    summary_ref[...] = lax.dot_general(
+        pick,
+        res[:, 0, span:],
+        (((1,), (1,)), ((), ())),
+        preferred_element_type=jnp.float32,
+        precision=lax.Precision.HIGHEST,
+    )[:4]
     reports.wait()
     if slots > 1:
         pltpu.make_async_copy(others, others, res_send_sem).wait()
@@ -412,7 +436,7 @@
         out_specs=[pl.BlockSpec(memory_space=pltpu.HBM), vmem],
         out_shape=[
             jax.ShapeDtypeStruct((intervals, 4, blocks * LANES), jnp.float32),
-            jax.ShapeDtypeStruct((intervals, 1, LANES), jnp.float32),
+            jax.ShapeDtypeStruct((4, intervals), jnp.float32),
         ],
         scratch_shapes=[pltpu.VMEM(a.shape, a.dtype) for k, a in enumerate(operands) if k != 10]
         + [pltpu.VMEM((pair, tile, w.shape[1]), jnp.bfloat16) for w in weights]
@@ -435,7 +459,7 @@
         ),
         name="report",
     )(*operands)
-    return stats, summary[:, 0, :4]
+    return stats, summary.T
 
 
 def solution(mesh):

time: 49.6 us -> 46.4 us (0.935)
  Pallas kernels: 44.8 us -> 41.6 us
    pallas_call x1, Pallas kernels: 44.8 us -> 41.6 us  [on_device(): pl.pallas_call(functools.partial(report_kernel, sizes, slots), in_specs=i...]
    slice x1 -> x0, local copies, waits for them, and re-layouts: 1.35 us -> none  [on_device(): return (stats, summary[:, 0, :4])]
    unnamed x1 -> x2, local copies, waits for them, and re-layouts: 1.67 us -> 2.92 us
where the time goes in v4:
time: 46.4 us; the launch traced here: 45.9 us
  Pallas kernels  41.6 us (90%)
  local copies, waits for them, and re-layouts  2.92 us (6%)
  between operations  1.29 us (3%)
    pallas_call x1, Pallas kernels, on_device(): pl.pallas_call(functools.partial(report_kernel, sizes, slots), in_specs=i...  41.6 us
    unnamed x2, local copies, waits for them, and re-layouts  2.92 us

profile of v4, /device:TPU:1, one launch (start us, length us, event | category | flops | bytes accessed | tf_op | source)
XLA Modules:
  0.0 45.9 jit_solution(14702389231517685430)
XLA Ops:
  1.3 41.6 %report.1 = (f32[16,4,1024]{2,1,0:T(4,128)}, f32[4,16]{1,0:T(4,128)}) custom-call(bf16[8,512,512]{2,1,0:T(8,128)(2,1)} %bitcast.7, bf16[512,1024]{1,0:T(8,128)(2,1)} %w1_hbm.1, f32[1,1024]{1,0:T(1,128)} %bitcast.8, bf16[1024,1024]{1,0:T(8,128)(2,1)} %w2_hbm.1, f32[1,1024]{1,0:T(1,128)} %bitcast.9, bf16[1024,512]{1,0:T(8,128)(2,1)} %w3_hbm.1, ...), custom_call_target="tpu_custom_call" | custom-call | tf_op jit(solution)/shard_map/report/pallas_call | solution.py:433
  42.9 1.7 %copy.18 = f32[16,4,1024]{2,1,0:T(4,128)} copy(f32[16,4,1024]{2,1,0:T(4,128)} %get-tuple-element.8) | data formatting | bytes 524288
  44.6 1.2 %copy.19 = f32[16,4]{0,1:T(4,128)} copy(f32[16,4]{0,1:T(4,128)} %bitcast.11) | data formatting | bytes 512

commit v5 on v4

--- a/solution.py
+++ b/solution.py
@@ -198,9 +198,20 @@
     turns = next(b for b in (max(8 // reps, 1), 1) if slots % b == 0)
     sources = [(t, n) for t in range(turns) for n in range(reps)]
     width = len(sources) * per * LANES
-    low_ids = lax.broadcasted_iota(jnp.int32, (LANES, LANES), 1)
-    high_ids = lax.broadcasted_iota(jnp.int32, (HIGHS, width), 0)
-    block_ids = lax.broadcasted_iota(jnp.int32, (blocks, width), 0) + x * blocks
+    half = jnp.bfloat16
+    tall = max(blocks, 16)
+    step_ids = lax.broadcasted_iota(jnp.int32, (16, width), 0)
+
+    def rows_of(row):
+        return jnp.broadcast_to(row, (16, width)).astype(half)
+
+    def spread(ids, first, count, values):
+        masks = [
+            (step_ids + (first + r)).astype(jnp.float32).astype(half) == ids
+            for r in range(0, count, 16)
+        ]
+        zero = jnp.zeros((16, width), half)
+        return [jnp.where(mask, value, zero) for value in values for mask in masks]
 
     def measure_all():
         logit = got[:, :, 0]
@@ -213,8 +224,6 @@
 
     def add(step, carry):
         first = step * turns
-        ids = jnp.concatenate([got[first + t, n, 1] for t, n in sources], axis=0)
-        down = jnp.transpose(ids).astype(jnp.int32) & (LANES - 1)
         out = []
         for e in range(held):
 
@@ -228,32 +237,25 @@
                     axis=1,
                 )
 
-            columns = [
-                q * lines + row
-                for q in range(len(sources))
-                for row in range(e * per, (e + 1) * per)
-            ]
+            bucket = line(got, 1).astype(jnp.int32)
+            low = rows_of((bucket & (LANES - 1)).astype(jnp.float32))
+            high = rows_of(
+                lax.shift_right_logical(bucket, LANES.bit_length() - 1).astype(jnp.float32)
+            )
+            observed = line(got, 2)
+            labels = [rows_of(observed), rows_of(1.0 - observed)]
+            values = [rows_of(line(vals, k)) for k in range(3)]
             one_hot = jnp.concatenate(
-                [jnp.where(low_ids == down[:, c : c + 1], 1.0, 0.0) for c in columns], axis=0
-            ).astype(jnp.bfloat16)
-            bucket = line(got, 1).astype(jnp.int32)
-            observed = line(got, 2)
-            high = lax.shift_right_logical(bucket, LANES.bit_length() - 1)
-            at_high = high_ids == high
-            at_block = block_ids == high
-            parts = [
-                jnp.where(at_high, observed, 0.0),
-                jnp.where(at_high, 1.0 - observed, 0.0),
-            ]
-            lower = []
-            for k in range(3):
-                value = line(vals, k)
-                upper = value.astype(jnp.bfloat16).astype(jnp.float32)
-                parts.append(jnp.where(at_block, upper, 0.0))
-                lower.append(jnp.where(at_block, value - upper, 0.0))
-            left = jnp.concatenate(parts + lower, axis=0).astype(jnp.bfloat16)
+                spread(low, 0, LANES, [jnp.ones((16, width), half)]), axis=0
+            )
+            left = jnp.concatenate(
+                spread(high, 0, HIGHS, labels) + spread(high, x * blocks, tall, values), axis=0
+            )
             out.append(
-                carry[e] + jnp.dot(left, one_hot, preferred_element_type=jnp.float32)
+                carry[e]
+                + lax.dot_general(
+                    left, one_hot, (((1,), (1,)), ((), ())), preferred_element_type=jnp.float32
+                )
             )
         return tuple(out)
 
@@ -299,19 +301,6 @@
     lane_ids = lax.broadcasted_iota(jnp.int32, (8, LANES), 1)
     bound = devices * per * LANES
 
-    def share(at):
-        @pl.loop(1, slots)
-        def _(k):
-            d = x * group + own_copy * slots + lax.rem(slot + k, slots)
-            pltpu.make_async_remote_copy(
-                src_ref=res.at[at],
-                dst_ref=res.at[at],
-                send_sem=res_send_sem,
-                recv_sem=res_recv_sem,
-                device_id=place(d),
-                device_id_type=MESH,
-            ).start()
-
     for i in range(held):
         total = totals[i]
         at = slot * held + i
@@ -321,10 +310,8 @@
         count = jnp.maximum(positives + negatives, 1.0)
         report = [positives / count]
         for k in range(3):
-            first = 2 * HIGHS + k * blocks
-            second = first + 3 * blocks
-            value = total[first : first + blocks] + total[second : second + blocks]
-            report.append(value / count)
+            first = 2 * HIGHS + k * tall
+            report.append(total[first : first + blocks] / count)
         for k in range(4):
             res[at, k : k + 1, 0:span] = jnp.concatenate(
                 [report[k][h : h + 1] for h in range(blocks)], axis=1
@@ -355,7 +342,20 @@
         line = jnp.where(lane_ids == 2, s_p / jnp.maximum(p_sum, 1.0), line)
         line = jnp.where(lane_ids == 3, s_sq / examples, line)
         res[at, :, span:] = line[0:4]
-        share(at)
+
+    own = pl.ds(slot * held, held)
+
+    @pl.loop(1, slots)
+    def _(k):
+        d = x * group + own_copy * slots + lax.rem(slot + k, slots)
+        pltpu.make_async_remote_copy(
+            src_ref=res.at[own],
+            dst_ref=res.at[own],
+            send_sem=res_send_sem,
+            recv_sem=res_recv_sem,
+            device_id=place(d),
+            device_id_type=MESH,
+        ).start()
 
     others = res.at[pl.ds(0, intervals - held)]
     if slots > 1:
@@ -383,6 +383,17 @@
         if count:
             sent = got.at[i, pl.ds(0, count)]
             pltpu.make_async_copy(sent, sent, send_sem.at[i]).wait()
+
+
+def finish_kernel(stats_in, summary_in, stats_ref, summary_ref, sems):
+    copies = [
+        pltpu.make_async_copy(stats_in, stats_ref, sems.at[0]),
+        pltpu.make_async_copy(summary_in, summary_ref, sems.at[1]),
+    ]
+    for copy in copies:
+        copy.start()
+    for copy in copies:
+        copy.wait()
 
 
 def on_device(sizes, *args):
@@ -444,7 +455,7 @@
             pltpu.VMEM((slots, 3, lines, LANES), jnp.float32),
             pltpu.VMEM((slots, reps, 3, lines, LANES), jnp.float32),
             pltpu.VMEM((slots, reps, 3, lines, LANES), jnp.float32),
-            pltpu.VMEM((held, 2 * HIGHS + 6 * blocks, LANES), jnp.float32),
+            pltpu.VMEM((held, 2 * HIGHS + 3 * max(blocks, 16), LANES), jnp.float32),
             pltpu.VMEM((intervals, 4, (blocks + 1) * LANES), jnp.float32),
             pltpu.SemaphoreType.DMA((slots,)),
             pltpu.SemaphoreType.DMA((11,)),
@@ -459,6 +470,16 @@
         ),
         name="report",
     )(*operands)
+    hbm = pl.BlockSpec(memory_space=pltpu.HBM)
+    stats, summary = pl.pallas_call(
+        finish_kernel,
+        in_specs=[hbm, hbm],
+        out_specs=[hbm, hbm],
+        out_shape=[jax.ShapeDtypeStruct(a.shape, a.dtype) for a in (stats, summary)],
+        scratch_shapes=[pltpu.SemaphoreType.DMA((2,))],
+        compiler_params=pltpu.CompilerParams(vmem_limit_bytes=60 * 2**20),
+        name="finish",
+    )(stats, summary)
     return stats, summary.T
 
 

time: 46.4 us -> 50 us (1.078)
  Pallas kernels: 41.6 us -> 48.5 us
  local copies, waits for them, and re-layouts: 2.92 us -> 0 us
    pallas_call x0 -> x1, Pallas kernels: none -> 9.12 us  [on_device(): pl.pallas_call(finish_kernel, in_specs=[hbm, hbm], out_specs=[hbm, hbm],...]
    unnamed x2 -> x0, local copies, waits for them, and re-layouts: 2.92 us -> none
    pallas_call x1, Pallas kernels: 41.6 us -> 39.4 us  [on_device(): pl.pallas_call(functools.partial(report_kernel, sizes, slots), in_specs=i...]
where the time goes in v5:
time: 50 us; the launch traced here: 49.8 us
  Pallas kernels  48.5 us (97%)
  between operations  1.29 us (3%)
    pallas_call x1, Pallas kernels, on_device(): pl.pallas_call(functools.partial(report_kernel, sizes, slots), in_specs=i...  39.4 us
    pallas_call x1, Pallas kernels, on_device(): pl.pallas_call(finish_kernel, in_specs=[hbm, hbm], out_specs=[hbm, hbm],...  9.12 us

profile of v5, /device:TPU:1, one launch (start us, length us, event | category | flops | bytes accessed | tf_op | source)
XLA Modules:
  0.0 49.8 jit_solution(12712014254262138267)
XLA Ops:
  1.3 39.4 %report.1 = (f32[16,4,1024]{2,1,0:T(4,128)}, f32[4,16]{1,0:T(4,128)}) custom-call(bf16[8,512,512]{2,1,0:T(8,128)(2,1)} %bitcast.7, bf16[512,1024]{1,0:T(8,128)(2,1)} %w1_hbm.1, f32[1,1024]{1,0:T(1,128)} %bitcast.8, bf16[1024,1024]{1,0:T(8,128)(2,1)} %w2_hbm.1, f32[1,1024]{1,0:T(1,128)} %bitcast.9, bf16[1024,512]{1,0:T(8,128)(2,1)} %w3_hbm.1, ...), custom_call_target="tpu_custom_call" | custom-call | tf_op jit(solution)/shard_map/report/pallas_call | solution.py:444
  40.7 9.1 %finish.1 = (f32[16,4,1024]{2,1,0:T(4,128)}, f32[4,16]{1,0:T(4,128)}) custom-call(f32[16,4,1024]{2,1,0:T(4,128)} %get-tuple-element.6.stats_in, f32[4,16]{1,0:T(4,128)} %get-tuple-element.7.summary_in), custom_call_target="tpu_custom_call" | custom-call | tf_op jit(solution)/shard_map/finish/pallas_call | solution.py:474

commit v6 on v5

--- a/solution.py
+++ b/solution.py
@@ -473,7 +473,7 @@
     hbm = pl.BlockSpec(memory_space=pltpu.HBM)
     stats, summary = pl.pallas_call(
         finish_kernel,
-        in_specs=[hbm, hbm],
+        in_specs=[vmem, vmem],
         out_specs=[hbm, hbm],
         out_shape=[jax.ShapeDtypeStruct(a.shape, a.dtype) for a in (stats, summary)],
         scratch_shapes=[pltpu.SemaphoreType.DMA((2,))],

time: 50 us -> 42.5 us (0.85)
  Pallas kernels: 48.5 us -> 41.1 us
    pallas_call x1, Pallas kernels: 9.12 us -> 1.67 us  [on_device(): pl.pallas_call(finish_kernel, in_specs=[vmem, vmem], out_specs=[hbm, hbm]...]
where the time goes in v6:
time: 42.5 us; the launch traced here: 42.4 us
  Pallas kernels  41.1 us (97%)
  between operations  1.29 us (3%)
    pallas_call x1, Pallas kernels, on_device(): pl.pallas_call(functools.partial(report_kernel, sizes, slots), in_specs=i...  39.4 us
    pallas_call x1, Pallas kernels, on_device(): pl.pallas_call(finish_kernel, in_specs=[vmem, vmem], out_specs=[hbm, hbm]...  1.67 us

profile of v6, /device:TPU:1, one launch (start us, length us, event | category | flops | bytes accessed | tf_op | source)
XLA Modules:
  0.0 42.4 jit_solution(11381272179509933856)
XLA Ops:
  1.3 39.4 %report.1 = (f32[16,4,1024]{2,1,0:T(4,128)}, f32[4,16]{1,0:T(4,128)}) custom-call(bf16[8,512,512]{2,1,0:T(8,128)(2,1)} %bitcast.7, bf16[512,1024]{1,0:T(8,128)(2,1)} %w1_hbm.1, f32[1,1024]{1,0:T(1,128)} %bitcast.8, bf16[1024,1024]{1,0:T(8,128)(2,1)} %w2_hbm.1, f32[1,1024]{1,0:T(1,128)} %bitcast.9, bf16[1024,512]{1,0:T(8,128)(2,1)} %w3_hbm.1, ...), custom_call_target="tpu_custom_call" | custom-call | tf_op jit(solution)/shard_map/report/pallas_call | solution.py:444
  40.7 1.7 %finish.1 = (f32[16,4,1024]{2,1,0:T(4,128)}, f32[4,16]{1,0:T(4,128)}) custom-call(f32[16,4,1024]{2,1,0:T(4,128)} %get-tuple-element.6.stats_in, f32[4,16]{1,0:T(4,128)} %get-tuple-element.7.summary_in), custom_call_target="tpu_custom_call" | custom-call | tf_op jit(solution)/shard_map/finish/pallas_call | solution.py:474
